TPU v7x, 32 devices: a whole 2x2x4 slice. The times are simulated.
32 devices in a mesh: shard: 4 (over y, core), rep: 8 (over z, x).
Axes of the slice: x: 2, y: 2, z: 4, core: 2. Of those that a mesh axis runs over, the one named last changes fastest.
Arguments:
- tokens: bfloat16 [16384, 896], P(('shard', 'rep')), may hold values from -6 to 6
- out_grad: bfloat16 [16384, 896], P(('shard', 'rep')), may hold values from -6 to 6
- segments: int32 [32, 512], P(('shard', 'rep')), may hold values from 0 to 7, never falling along the last dimension, each value on 1 to 256 neighbouring positions
- w_query: float32 [896, 896], P('shard'), may hold values from -0.1875 to 0.1875
- w_key: float32 [896, 128], P('shard'), may hold values from -0.1875 to 0.1875
- w_value: float32 [896, 128], P('shard'), may hold values from -0.1875 to 0.1875
- w_out: float32 [896, 896], P('shard'), may hold values from -0.75 to 0.75
- w_gate: float32 [896, 4864], P('shard'), may hold values from -0.1875 to 0.1875
- w_up: float32 [896, 4864], P('shard'), may hold values from -0.1875 to 0.1875
- w_down: float32 [4864, 896], P('shard'), may hold values from -0.078125 to 0.078125
- gains: float32 [2, 896], P(None, 'shard'), may hold values from 0.5 to 1.5
- biases: float32 [1152], P('shard'), may hold values from -3 to 3
- mom_query: float32 [896, 896], P('shard'), may hold values from -768 to 768
- mom_key: float32 [896, 128], P('shard'), may hold values from -768 to 768
- mom_value: float32 [896, 128], P('shard'), may hold values from -768 to 768
- mom_out: float32 [896, 896], P('shard'), may hold values from -160 to 160
- mom_gate: float32 [896, 4864], P('shard'), may hold values from -192 to 192
- mom_up: float32 [896, 4864], P('shard'), may hold values from -192 to 192
- mom_down: float32 [4864, 896], P('shard'), may hold values from -384 to 384
- gain_mom: float32 [2, 896], P(None, 'shard'), may hold values from -768 to 768
- bias_mom: float32 [1152], P('shard'), may hold values from -768 to 768
Outputs:
- result: bfloat16 [16384, 896], P(('shard', 'rep'))
- input_grad: float32 [16384, 896], P(('shard', 'rep'))
- mom_query_new: float32 [896, 896], P('shard')
- mom_key_new: float32 [896, 128], P('shard')
- mom_value_new: float32 [896, 128], P('shard')
- mom_out_new: float32 [896, 896], P('shard')
- mom_gate_new: float32 [896, 4864], P('shard')
- mom_up_new: float32 [896, 4864], P('shard')
- mom_down_new: float32 [4864, 896], P('shard')
- weight_query_new: float32 [896, 896], P('shard')
- weight_key_new: float32 [896, 128], P('shard')
- weight_value_new: float32 [896, 128], P('shard')
- weight_out_new: float32 [896, 896], P('shard')
- weight_gate_new: float32 [896, 4864], P('shard')
- weight_up_new: float32 [896, 4864], P('shard')
- weight_down_new: float32 [4864, 896], P('shard')
- gain_mom_new: float32 [2, 896], P(None, 'shard')
- gains_new: float32 [2, 896], P(None, 'shard')
- bias_mom_new: float32 [1152], P('shard')
- biases_new: float32 [1152], P('shard')
Inputs may be any that keep to these rules, and one draw needn't show every extreme that they name: `segments`: segment numbers never fall along a row; a document holds at most 256 tokens.
All inputs are finite; a program needn't handle non-finite values.
Results may differ from a plain program's by a relative error of at most 0.012.
The roundings to bfloat16 on the way count: a program that leaves them out, or rounds other values in their place, can miss the bound.
Values may be sent and summed in bfloat16 or wider, within the bound.
A program may use at most 448 MiB of HBM per device.

v0:
```python
import math

import jax
import jax.numpy as jnp
from jax import lax
from jax.sharding import PartitionSpec as P

D = 896
QH = 14
KVH = 2
HD = 64
NS_ITERS = 5


eps_norm = 1e-06
theta_base = 1000000.0
coef_a = 3.4445
coef_b = -4.775
coef_c = 2.0315
momentum_decay = 0.9
muon_rate = 1.0
vector_rate = 0.1
masked_score = -1000000000.0
highest = lax.Precision.HIGHEST


def for_sending(array):

    def short(part):
        return part.astype(jnp.bfloat16) if part.dtype == jnp.float32 else part

    return jax.tree.map(short, array)


def product(left, right):
    return jnp.dot(left, right, preferred_element_type=jnp.float32)


def left_product(left, right):
    return lax.dot_general(
        left, right, (((0,), (0,)), ((), ())), preferred_element_type=jnp.float32
    )


def right_product(left, right):
    return lax.dot_general(
        left, right, (((1,), (1,)), ((), ())), preferred_element_type=jnp.float32
    )


def rope_tables(segments, head):
    length = segments.shape[-1]
    indices = jnp.arange(length, dtype=jnp.int32)
    first = jnp.ones(segments.shape[:-1] + (1,), dtype=jnp.bool_)
    change = jnp.concatenate([first, segments[..., 1:] != segments[..., :-1]], axis=-1)
    starts = lax.cummax(jnp.where(change, indices, 0), axis=segments.ndim - 1)
    place = (indices - starts).astype(jnp.float32)
    half_dim = head // 2
    inverse = jnp.exp(
        jnp.arange(half_dim, dtype=jnp.float32) * (-2.0 * math.log(theta_base) / head)
    )
    angles = place[..., None] * inverse
    angles = jnp.concatenate([angles, angles], axis=-1)
    return (jnp.cos(angles), jnp.sin(angles))


def rotary(values, cosine, sine):
    half_dim = values.shape[-1] // 2
    turned = jnp.concatenate([-values[..., half_dim:], values[..., :half_dim]], axis=-1)
    return values * cosine + turned * sine


def unrotary(grads, cosine, sine):
    half_dim = grads.shape[-1] // 2
    scaled = grads * sine
    turned = jnp.concatenate([scaled[..., half_dim:], -scaled[..., :half_dim]], axis=-1)
    return grads * cosine + turned


def norm_rows(values, gain):
    factor = lax.rsqrt(jnp.mean(values * values, axis=-1, keepdims=True) + eps_norm)
    unit = values * factor
    return (unit, factor, (unit * gain).astype(jnp.bfloat16))


def norm_back(grad_out, unit, factor, gain):
    grad_unit = grad_out * gain
    grad_gain = jnp.sum(grad_out * unit, axis=0)
    grad_in = factor * (grad_unit - unit * jnp.mean(grad_unit * unit, axis=-1, keepdims=True))
    return (grad_in, grad_gain)


def orthogonal_part(matrix):
    tall = matrix.shape[0] > matrix.shape[1]
    work = matrix.T if tall else matrix
    work = work / (jnp.sqrt(jnp.sum(work * work)) + 1e-07)
    for turn in range(NS_ITERS):
        square = jnp.dot(work, work.T, precision=highest)
        mixed = coef_b * square + coef_c * jnp.dot(square, square, precision=highest)
        work = coef_a * work + jnp.dot(mixed, work, precision=highest)
    return work.T if tall else work


def owner_work(slots, shapes, group, widest):

    def compute(incoming):
        columns = []
        filled = 0
        for index, offset in slots:
            rows, cols = shapes[index]
            count = rows * cols
            whole = incoming[:, offset : offset + count].reshape(group * rows, cols)
            factor = muon_rate * math.sqrt(max(group * rows, cols) / (group * rows))
            stepped = factor * orthogonal_part(whole)
            columns.append(stepped.reshape(group, count))
            filled = filled + count
        columns.append(jnp.zeros((group, widest - filled), jnp.float32))
        return jnp.concatenate(columns, axis=1)

    return compute


def local(
    tokens,
    out_grad,
    segments,
    w_query,
    w_key,
    w_value,
    w_out,
    w_gate,
    w_up,
    w_down,
    gains,
    biases,
    mom_query,
    mom_key,
    mom_value,
    mom_out,
    mom_gate,
    mom_up,
    mom_down,
    gain_mom,
    bias_mom,
):
    group = lax.axis_size("shard")
    replicas = lax.axis_size("rep")
    kv_width = KVH * HD
    length = tokens.shape[0]
    low_query = w_query.astype(jnp.bfloat16)
    low_key = w_key.astype(jnp.bfloat16)
    low_value = w_value.astype(jnp.bfloat16)
    low_out = w_out.astype(jnp.bfloat16)
    low_gate = w_gate.astype(jnp.bfloat16)
    low_up = w_up.astype(jnp.bfloat16)
    low_down = w_down.astype(jnp.bfloat16)
    low_gains = gains.astype(jnp.bfloat16)
    low_biases = biases.astype(jnp.bfloat16)
    fetched = (
        lax.all_gather(low_query, "shard", axis=0, tiled=True),
        lax.all_gather(low_key, "shard", axis=0, tiled=True),
        lax.all_gather(low_value, "shard", axis=0, tiled=True),
        lax.all_gather(low_out, "shard", axis=0, tiled=True),
        lax.all_gather(low_gate, "shard", axis=0, tiled=True),
        lax.all_gather(low_up, "shard", axis=0, tiled=True),
        lax.all_gather(low_down, "shard", axis=0, tiled=True),
        lax.all_gather(low_gains, "shard", axis=1, tiled=True),
        lax.all_gather(low_biases, "shard", axis=0, tiled=True),
    )
    (
        full_query,
        full_key,
        full_value,
        full_out,
        full_gate,
        full_up,
        full_down,
        full_gains,
        full_biases,
    ) = fetched
    inputs = tokens.astype(jnp.float32)
    gain_one = full_gains[0].astype(jnp.float32)
    gain_two = full_gains[1].astype(jnp.float32)
    bias_all = full_biases.astype(jnp.float32)
    unit_one, factor_one, normed_one = norm_rows(inputs, gain_one)
    query_lin = product(normed_one, full_query) + bias_all[:D]
    key_lin = product(normed_one, full_key) + bias_all[D : D + kv_width]
    value_lin = product(normed_one, full_value) + bias_all[D + kv_width :]
    seg_row = segments[0]
    cosine, sine = rope_tables(seg_row, HD)
    cosine = cosine[:, None, :]
    sine = sine[:, None, :]
    queries = rotary(query_lin.reshape(length, QH, HD), cosine, sine).astype(jnp.bfloat16)
    keys = rotary(key_lin.reshape(length, KVH, HD), cosine, sine).astype(jnp.bfloat16)
    values = value_lin.astype(jnp.bfloat16).reshape(length, KVH, HD)
    grouped = queries.reshape(length, KVH, QH // KVH, HD)
    score_scale = 1.0 / math.sqrt(HD)
    places = jnp.arange(length)
    allowed = (places[:, None] >= places[None, :]) & (seg_row[:, None] == seg_row[None, :])
    scores = (
        jnp.einsum("qhgd,khd->hgqk", grouped, keys, preferred_element_type=jnp.float32)
        * score_scale
    )
    probs = jax.nn.softmax(jnp.where(allowed, scores, masked_score), axis=-1)
    probs_low = probs.astype(jnp.bfloat16)
    attended = jnp.einsum("hgqk,khd->qhgd", probs_low, values, preferred_element_type=jnp.float32)
    attended = attended.reshape(length, D).astype(jnp.bfloat16)
    middle = inputs + product(attended, full_out)
    unit_two, factor_two, normed_two = norm_rows(middle, gain_two)
    gate_val = product(normed_two, full_gate)
    up_val = product(normed_two, full_up)
    sigma = jax.nn.sigmoid(gate_val)
    swish = gate_val * sigma
    hidden = (swish * up_val).astype(jnp.bfloat16)
    result = (middle + product(hidden, full_down)).astype(jnp.bfloat16)
    again = (
        lax.all_gather(low_query, "shard", axis=0, tiled=True),
        lax.all_gather(low_key, "shard", axis=0, tiled=True),
        lax.all_gather(low_value, "shard", axis=0, tiled=True),
        lax.all_gather(low_out, "shard", axis=0, tiled=True),
        lax.all_gather(low_gate, "shard", axis=0, tiled=True),
        lax.all_gather(low_up, "shard", axis=0, tiled=True),
        lax.all_gather(low_down, "shard", axis=0, tiled=True),
        lax.all_gather(low_gains, "shard", axis=1, tiled=True),
    )
    back_query, back_key, back_value, back_out, back_gate, back_up, back_down, back_gains = again
    gain_one_back = back_gains[0].astype(jnp.float32)
    gain_two_back = back_gains[1].astype(jnp.float32)
    cotangent = out_grad.astype(jnp.float32)
    grad_down = left_product(hidden, out_grad)
    dhidden = right_product(out_grad, back_down)
    dgate = (dhidden * up_val * sigma * (1.0 + gate_val * (1.0 - sigma))).astype(jnp.bfloat16)
    dup = (dhidden * swish).astype(jnp.bfloat16)
    grad_gate = left_product(normed_two, dgate)
    grad_up = left_product(normed_two, dup)
    dnormed_two = right_product(dgate, back_gate) + right_product(dup, back_up)
    dmiddle_norm, grad_gain_two = norm_back(dnormed_two, unit_two, factor_two, gain_two_back)
    dmiddle = cotangent + dmiddle_norm
    dmid_low = dmiddle.astype(jnp.bfloat16)
    grad_out = left_product(attended, dmid_low)
    dattended = (
        right_product(dmid_low, back_out).astype(jnp.bfloat16).reshape(length, KVH, QH // KVH, HD)
    )
    dvalues = jnp.einsum("hgqk,qhgd->khd", probs_low, dattended, preferred_element_type=jnp.float32)
    dvalues = dvalues.reshape(length, kv_width).astype(jnp.bfloat16)
    dprobs = jnp.einsum("qhgd,khd->hgqk", dattended, values, preferred_element_type=jnp.float32)
    dscores = (
        probs * (dprobs - jnp.sum(probs * dprobs, axis=-1, keepdims=True)) * score_scale
    ).astype(jnp.bfloat16)
    dquery = jnp.einsum(
        "hgqk,khd->qhgd", dscores, keys, preferred_element_type=jnp.float32
    ).reshape(length, QH, HD)
    dkey = jnp.einsum("hgqk,qhgd->khd", dscores, grouped, preferred_element_type=jnp.float32)
    dquery = unrotary(dquery, cosine, sine).reshape(length, D).astype(jnp.bfloat16)
    dkey = unrotary(dkey, cosine, sine).reshape(length, kv_width).astype(jnp.bfloat16)
    grad_query = left_product(normed_one, dquery)
    grad_key = left_product(normed_one, dkey)
    grad_value = left_product(normed_one, dvalues)
    grad_biases = jnp.concatenate(
        [
            jnp.sum(dquery.astype(jnp.float32), axis=0),
            jnp.sum(dkey.astype(jnp.float32), axis=0),
            jnp.sum(dvalues.astype(jnp.float32), axis=0),
        ]
    )
    dnormed_one = (
        right_product(dquery, back_query)
        + right_product(dkey, back_key)
        + right_product(dvalues, back_value)
    )
    dinput_norm, grad_gain_one = norm_back(dnormed_one, unit_one, factor_one, gain_one_back)
    input_grad = dmiddle + dinput_norm
    grad_gains = jnp.stack([grad_gain_one, grad_gain_two])
    (
        part_query,
        part_key,
        part_value,
        part_out,
        part_gate,
        part_up,
        part_down,
        part_gains,
        part_biases,
    ) = (
        lax.psum_scatter(grad_query, "shard", scatter_dimension=0, tiled=True),
        lax.psum_scatter(grad_key, "shard", scatter_dimension=0, tiled=True),
        lax.psum_scatter(grad_value, "shard", scatter_dimension=0, tiled=True),
        lax.psum_scatter(grad_out, "shard", scatter_dimension=0, tiled=True),
        lax.psum_scatter(grad_gate, "shard", scatter_dimension=0, tiled=True),
        lax.psum_scatter(grad_up, "shard", scatter_dimension=0, tiled=True),
        lax.psum_scatter(grad_down, "shard", scatter_dimension=0, tiled=True),
        lax.psum_scatter(grad_gains, "shard", scatter_dimension=1, tiled=True),
        lax.psum_scatter(grad_biases, "shard", scatter_dimension=0, tiled=True),
    )
    summed = lax.psum(
        (
            part_query,
            part_key,
            part_value,
            part_out,
            part_gate,
            part_up,
            part_down,
            part_gains,
            part_biases,
        ),
        "rep",
    )
    sum_query, sum_key, sum_value, sum_out, sum_gate, sum_up, sum_down, sum_gains, sum_biases = (
        summed
    )
    new_query = momentum_decay * mom_query + sum_query
    new_key = momentum_decay * mom_key + sum_key
    new_value = momentum_decay * mom_value + sum_value
    new_out = momentum_decay * mom_out + sum_out
    new_gate = momentum_decay * mom_gate + sum_gate
    new_up = momentum_decay * mom_up + sum_up
    new_down = momentum_decay * mom_down + sum_down
    token_total = length * group * replicas
    gain_mom_new = momentum_decay * gain_mom + sum_gains
    gains_new = gains - vector_rate * gain_mom_new / math.sqrt(token_total)
    bias_mom_new = momentum_decay * bias_mom + sum_biases
    biases_new = biases - vector_rate * bias_mom_new / math.sqrt(token_total)
    ordered = [new_gate, new_up, new_down, new_query, new_out, new_key, new_value]
    masters_ordered = [w_gate, w_up, w_down, w_query, w_out, w_key, w_value]
    shard_shapes_ordered = [item.shape for item in ordered]
    counts = [item.shape[0] * item.shape[1] for item in ordered]
    layout = []
    place_of = {}
    widest = 1
    for owner in range(group):
        offset = 0
        slots = []
        for index in range(len(ordered)):
            if index % group == owner:
                slots.append((index, offset))
                place_of[index] = offset
                offset = offset + counts[index]
        layout.append(slots)
        widest = max(widest, offset)
    send_rows = []
    for slots in layout:
        flat_pieces = [ordered[index].reshape(-1) for index, offset in slots]
        filled = sum((counts[index] for index, offset in slots))
        flat_pieces.append(jnp.zeros((widest - filled,), jnp.float32))
        send_rows.append(jnp.concatenate(flat_pieces))
    outgoing = jnp.stack(send_rows)
    incoming = lax.all_to_all(outgoing, "shard", split_axis=0, concat_axis=0, tiled=True)
    branches = [owner_work(slots, shard_shapes_ordered, group, widest) for slots in layout]
    outcome = lax.switch(lax.axis_index("shard"), branches, incoming)
    returned = jax.tree.map(
        lambda part, own: part.astype(own.dtype),
        lax.all_to_all(for_sending(outcome), "shard", split_axis=0, concat_axis=0, tiled=True),
        outcome,
    )
    updated = []
    for index in range(len(ordered)):
        owner = index % group
        start_at = place_of[index]
        piece = returned[owner, start_at : start_at + counts[index]].reshape(
            shard_shapes_ordered[index]
        )
        updated.append(masters_ordered[index] - piece)
    upd_gate, upd_up, upd_down, upd_query, upd_out, upd_key, upd_value = updated
    return (
        result,
        input_grad,
        new_query,
        new_key,
        new_value,
        new_out,
        new_gate,
        new_up,
        new_down,
        upd_query,
        upd_key,
        upd_value,
        upd_out,
        upd_gate,
        upd_up,
        upd_down,
        gain_mom_new,
        gains_new,
        bias_mom_new,
        biases_new,
    )


def solution(mesh):
    placed = (
        P(("shard", "rep"), None),
        P(("shard", "rep"), None),
        P(("shard", "rep"), None),
        P("shard", None),
        P("shard", None),
        P("shard", None),
        P("shard", None),
        P("shard", None),
        P("shard", None),
        P("shard", None),
        P(None, "shard"),
        P("shard"),
        P("shard", None),
        P("shard", None),
        P("shard", None),
        P("shard", None),
        P("shard", None),
        P("shard", None),
        P("shard", None),
        P(None, "shard"),
        P("shard"),
    )
    return jax.shard_map(
        local,
        mesh=mesh,
        in_specs=placed,
        out_specs=(
            P(("shard", "rep"), None),
            P(("shard", "rep"), None),
            P("shard", None),
            P("shard", None),
            P("shard", None),
            P("shard", None),
            P("shard", None),
            P("shard", None),
            P("shard", None),
            P("shard", None),
            P("shard", None),
            P("shard", None),
            P("shard", None),
            P("shard", None),
            P("shard", None),
            P("shard", None),
            P(None, "shard"),
            P(None, "shard"),
            P("shard"),
            P("shard"),
        ),
        check_vma=False,
    )
```

profile of v0, /device:TPU:0, one launch (start us, length us, event | category | flops | bytes accessed | tf_op | source)
XLA Modules:
  0.0 3064.6 jit_solution(4309162106371104474)
XLA Ops:
  85.7 32.6 %all-gather.13.cloned.1.call-done = bf16[896,4864]{1,0:T(8,128)(2,1)} async-done(((bf16[224,4864]{1,0:T(8,128)(2,1)}), bf16[896,4864]{1,0:T(8,128)(2,1)}) %all-gather.13.cloned.1.call-update) | async-done | bytes 8716304 | tf_op jit(solution)/shard_map/all_gather | solution.py:165
  129.9 50.6 %all-gather.11.cloned.1.call-done = bf16[896,4864]{1,0:T(8,128)(2,1)} async-done(((bf16[224,4864]{1,0:T(8,128)(2,1)}), bf16[896,4864]{1,0:T(8,128)(2,1)}) %all-gather.11.cloned.1.call-update) | async-done | bytes 8716304 | tf_op jit(solution)/shard_map/all_gather | solution.py:164
  192.2 50.5 %all-gather.15.cloned.1.call-done = bf16[4864,896]{1,0:T(8,128)(2,1)} async-done(((bf16[1216,896]{1,0:T(8,128)(2,1)}), bf16[4864,896]{1,0:T(8,128)(2,1)}) %all-gather.15.cloned.1.call-update) | async-done | bytes 8716304 | tf_op jit(solution)/shard_map/all_gather | solution.py:166
  242.7 19.0 multiply_convert_fusion
  308.7 22.6 broadcast_multiply_fusion.3
  338.2 19.7 fusion.267
  364.4 12.7 fusion.399
  401.0 37.8 %reduce-scatter.11.cloned.1.call-done = f32[224,896]{1,0:T(8,128)} async-done(((f32[896,896]{1,0:T(8,128)}), f32[224,896]{1,0:T(8,128)}) %reduce-scatter.11.cloned.1.call-update) | async-done | bytes 802832 | tf_op jit(solution)/shard_map/reduce_scatter | solution.py:285
  438.8 132.6 %reduce-scatter.23.cloned.1.call-done = f32[1216,896]{1,0:T(8,128)} async-done(((f32[4864,896]{1,0:T(8,128)}), f32[1216,896]{1,0:T(8,128)}) %reduce-scatter.23.cloned.1.call-update) | async-done | bytes 4358160 | tf_op jit(solution)/shard_map/reduce_scatter | solution.py:291
  571.4 133.0 %reduce-scatter.21.cloned.1.call-done = f32[224,4864]{1,0:T(8,128)} async-done(((f32[896,4864]{1,0:T(8,128)}), f32[224,4864]{1,0:T(8,128)}) %reduce-scatter.21.cloned.1.call-update) | async-done | bytes 4358160 | tf_op jit(solution)/shard_map/reduce_scatter | solution.py:290
  704.3 132.6 %reduce-scatter.19.cloned.1.call-done = f32[224,4864]{1,0:T(8,128)} async-done(((f32[896,4864]{1,0:T(8,128)}), f32[224,4864]{1,0:T(8,128)}) %reduce-scatter.19.cloned.1.call-update) | async-done | bytes 4358160 | tf_op jit(solution)/shard_map/reduce_scatter | solution.py:289
  837.0 472.9 %all-reduce.8.cloned.1.call-done = (f32[224,896]{1,0:T(8,128)}, f32[224,128]{1,0:T(8,128)}, f32[224,128]{1,0:T(8,128)}, f32[224,896]{1,0:T(8,128)}, f32[224,4864...) async-done(((f32[224,896]{1,0:T(8,128)}, f32[224,128]{1,0:T(8,128)}, f32[224,128]{1,0:T(8,128)}, f32[224,896]{1,0:T(8,128)}, f32[224,4864]{1,0:T(8,128)}, ...) | async-done | bytes 14909456 | tf_op jit(solution)/shard_map/psum | solution.py:295
  1354.0 20.9 pad_maximum_fusion.1
  1375.0 17.2 all_to_all.26
  1399.9 224.5 %all-to-all-done = f32[4,1,1290240]{2,1,0:T(1,128)} async-done(((f32[4,1,1290240]{2,1,0:T(1,128)}), f32[4,1,1290240]{2,1,0:T(1,128)}, u32[]{:S(2)}, u32[]{:S(2)}) %all-to-all-start) | async-done | bytes 20643872 | tf_op jit(solution)/shard_map/all_to_all | solution.py:348
  1624.3 17.7 copy.132
  1642.0 1069.1 %conditional.1 = (bf16[4,1290240]{1,0:T(4,128)(2,1)}) conditional(s32[]{:T(128)} %clamp.3, f32[4,1290240]{1,0:T(4,128)S(1)} %bitcast.451, f32[4,1290240]{1,0:T(4,128)S(1)} %bitcast.452, f32[4,1290240]{1,0:T(4,128)S(1)} %bitcast.453, f32[4,1290240]{1,0:T(4,128)S(1)} %bitcast.454), branch_computations={%region_23.26_spmd, %region_26.29_spmd, %region_29.32_spmd, %regio... | conditional | flops 641346568192 | bytes 977420416 | solution.py:350
  1667.2 13.1 slice_divide_fusion
  1680.3 51.4 %div.85 = f32[896,4864]{1,0:T(8,128)} reshape(f32[4,1089536]{1,0:T(4,128)} %slice_divide_fusion) | data formatting | bytes 34865152 | tf_op jit(solution)/shard_map/cond/branch_0_fun/div | solution.py:96
  1735.9 13.3 fusion.346
  1749.2 64.4 %fusion.336 = f32[896,896]{1,0:T(8,128)} fusion(f32[896,4864]{1,0:T(8,128)} %div.85), kind=kOutput, calls=%fused_computation.459 | convolution fusion | flops 46858764288 | bytes 20643840 | tf_op jit(solution)/shard_map/cond/branch_0_fun/dot_general | solution.py:98
  1813.6 15.8 fusion.337
  1829.4 65.5 %multiply_add_fusion.3 = f32[896,4864]{1,0:T(8,128)} fusion(f32[896,4864]{1,0:T(8,128)} %div.85, f32[896,896]{1,0:T(8,128)} %fusion.337, f32[896,896]{1,0:T(8,128)S(1)} %copy-done.15), kind=kOutput, calls=%fused_computation.5 | convolution fusion | flops 46869889024 | bytes 41287680 | tf_op jit(solution)/shard_map/cond/branch_0_fun/dot_general | solution.py:100
  1894.9 62.8 %fusion.338 = f32[896,896]{1,0:T(8,128)S(1)} fusion(f32[896,4864]{1,0:T(8,128)} %multiply_add_fusion.3), kind=kOutput, calls=%fused_computation.461 | convolution fusion | flops 46858764288 | bytes 20643840 | tf_op jit(solution)/shard_map/cond/branch_0_fun/dot_general | solution.py:98
  1957.6 13.1 fusion.339
  1970.7 65.4 %multiply_add_fusion.2 = f32[896,4864]{1,0:T(8,128)} fusion(f32[896,4864]{1,0:T(8,128)} %multiply_add_fusion.3, f32[896,896]{1,0:T(8,128)} %fusion.339, f32[896,896]{1,0:T(8,128)S(1)} %fusion.338), kind=kOutput, calls=%fused_computation.4 | convolution fusion | flops 46869889024 | bytes 41287680 | tf_op jit(solution)/shard_map/cond/branch_0_fun/dot_general | solution.py:100
  2036.2 62.8 %fusion.340 = f32[896,896]{1,0:T(8,128)S(1)} fusion(f32[896,4864]{1,0:T(8,128)} %multiply_add_fusion.2), kind=kOutput, calls=%fused_computation.463 | convolution fusion | flops 46858764288 | bytes 20643840 | tf_op jit(solution)/shard_map/cond/branch_0_fun/dot_general | solution.py:98
  2098.9 13.1 fusion.341
  2112.0 65.4 %multiply_add_fusion.1 = f32[896,4864]{1,0:T(8,128)} fusion(f32[896,4864]{1,0:T(8,128)} %multiply_add_fusion.2, f32[896,896]{1,0:T(8,128)} %fusion.341, f32[896,896]{1,0:T(8,128)S(1)} %fusion.340), kind=kOutput, calls=%fused_computation.3 | convolution fusion | flops 46869889024 | bytes 41287680 | tf_op jit(solution)/shard_map/cond/branch_0_fun/dot_general | solution.py:100
  2177.4 62.8 %fusion.342 = f32[896,896]{1,0:T(8,128)S(1)} fusion(f32[896,4864]{1,0:T(8,128)} %multiply_add_fusion.1), kind=kOutput, calls=%fused_computation.465 | convolution fusion | flops 46858764288 | bytes 20643840 | tf_op jit(solution)/shard_map/cond/branch_0_fun/dot_general | solution.py:98
  2240.2 13.1 fusion.343
  2253.3 65.4 %multiply_add_fusion = f32[896,4864]{1,0:T(8,128)} fusion(f32[896,4864]{1,0:T(8,128)} %multiply_add_fusion.1, f32[896,896]{1,0:T(8,128)} %fusion.343, f32[896,896]{1,0:T(8,128)S(1)} %fusion.342), kind=kOutput, calls=%fused_computation.2 | convolution fusion | flops 46869889024 | bytes 41287680 | tf_op jit(solution)/shard_map/cond/branch_0_fun/dot_general | solution.py:100
  2318.7 62.8 %fusion.344 = f32[896,896]{1,0:T(8,128)S(1)} fusion(f32[896,4864]{1,0:T(8,128)} %multiply_add_fusion), kind=kOutput, calls=%fused_computation.467 | convolution fusion | flops 46858764288 | bytes 20643840 | tf_op jit(solution)/shard_map/cond/branch_0_fun/dot_general | solution.py:98
  2381.5 13.1 fusion.345
  2394.6 65.7 %add_multiply_fusion = bf16[896,4864]{1,0:T(8,128)(2,1)} fusion(f32[896,4864]{1,0:T(8,128)} %multiply_add_fusion, f32[896,896]{1,0:T(8,128)} %fusion.345, f32[896,896]{1,0:T(8,128)S(1)} %fusion.344), kind=kOutput, calls=%fused_computation.1 | convolution fusion | flops 46878605312 | bytes 32571392 | tf_op jit(solution)/shard_map/cond/branch_0_fun/dot_general | solution.py:100
  2460.3 13.8 reshape.270
  2486.1 12.3 multiply_add_fusion.8
  2498.4 12.3 fusion.348
  2535.0 12.3 fusion.350
  2620.2 12.3 fusion.355
  2644.9 37.1 %pad_maximum_fusion = bf16[4,1290240]{1,0:T(4,128)(2,1)} fusion(bf16[4,200704]{1,0:T(4,128)(2,1)S(1)} %reshape.271, bf16[4,1089536]{1,0:T(4,128)(2,1)} %reshape.270), kind=kLoop, calls=%fused_computation | loop fusion | flops 20643840 | bytes 20643840 | tf_op jit(solution)/shard_map/cond/branch_0_fun/concatenate | solution.py:118
  2711.6 21.4 reduce.43
  2733.0 27.0 reshape.355
  2790.0 94.2 %all-reduce.3 = f32[1152]{0:T(1024)S(1)} all-reduce(f32[1152]{0:T(1024)S(1)} %pad_maximum_fusion.7), channel_id=10, replica_groups=mesh['shard'=4,'rep'=8] {'shard'}, use_global_device_ids=true, to_apply=%region_41.42.clone | all-reduce | flops 1152 | bytes 9216
  2885.3 18.3 all-reduce.4
  2904.8 24.7 reshape.356
  2929.5 17.7 copy.131
  2960.9 57.5 %slice_reduce_fusion = (f32[1089536]{0:T(1024)}, f32[1089536]{0:T(1024)}, f32[1089536]{0:T(1024)}) fusion(f32[4,1290240]{1,0:T(4,128)} %bitcast.459), kind=kLoop, calls=%fused_computation.340 | loop fusion | bytes 26148864 | tf_op jit(solution)/shard_map/slice | solution.py:360
  (318 shorter events, 470.5 us)
Async XLA Ops:
  7.2 47.2 %all-gather.7.cloned.1.call-start = ((), (), s32[]{:S(2)}) async-start(), calls=%async_computation.10 | async-start | bytes 2007040 | tf_op jit(solution)/shard_map/all_gather | solution.py:160
  9.2 72.0 %all-gather.9.cloned.1.call-start = ((), (), s32[]{:S(2)}) async-start(), calls=%async_computation.11 | async-start | bytes 2007040 | tf_op jit(solution)/shard_map/all_gather | solution.py:163
  11.2 107.2 %all-gather.13.cloned.1.call-start = ((), (), s32[]{:S(2)}) async-start(), calls=%async_computation.13 | async-start | bytes 10895360 | tf_op jit(solution)/shard_map/all_gather | solution.py:165
  15.1 165.5 %all-gather.11.cloned.1.call-start = ((), (), s32[]{:S(2)}) async-start(), calls=%async_computation.12 | async-start | bytes 10895360 | tf_op jit(solution)/shard_map/all_gather | solution.py:164
  19.0 10.9 copy-start.75
  19.0 20.0 copy-start.53
  19.0 20.1 copy-start.51
  19.0 223.7 %all-gather.15.cloned.1.call-start = ((), (), s32[]{:S(2)}) async-start(), calls=%async_computation.14 | async-start | bytes 10895360 | tf_op jit(solution)/shard_map/all_gather | solution.py:166
  23.3 29.3 copy-start.13
  23.3 377.6 %reduce-scatter.15.cloned.1.call-start = ((), (), s32[]{:S(2)}) async-start(), calls=%async_computation.17 | async-start | bytes 573440 | tf_op jit(solution)/shard_map/reduce_scatter | solution.py:287
  44.8 9.0 copy-start.42
  52.2 308.2 %copy-start.63 = (f32[896]{0:T(1024)}, f32[896]{0:T(1024)S(1)}, u32[]{:S(2)}) copy-start(f32[896]{0:T(1024)S(1)} %get-tuple-element.39) | copy-start | bytes 10756
  52.6 307.2 %copy-start.27 = (f32[512,64]{0,1:T(8,128)}, f32[512,64]{0,1:T(8,128)S(1)}, u32[]{:S(2)}) copy-start(f32[512,64]{0,1:T(8,128)S(1)} %get-tuple-element.82) | copy-start | bytes 393220
  52.9 307.5 %copy-start.65 = (f32[512]{0:T(512)}, f32[512]{0:T(512)S(1)}, u32[]{:S(2)}) copy-start(f32[512]{0:T(512)S(1)} %add_rsqrt_fusion.1) | copy-start | bytes 6148
  53.8 8.5 copy-start.57
  85.7 94.8 %copy-start.21 = (bf16[512,896]{1,0:T(8,128)(2,1)}, bf16[512,896]{1,0:T(8,128)(2,1)S(1)}, u32[]{:S(2)}) copy-start(bf16[512,896]{1,0:T(8,128)(2,1)S(1)} %multiply_convert_fusion.3) | copy-start | bytes 2752516
  129.9 112.8 %copy-start.39 = (bf16[512,896]{1,0:T(8,128)(2,1)S(1)}, bf16[512,896]{1,0:T(8,128)(2,1)}, u32[]{:S(2)}) copy-start(bf16[512,896]{1,0:T(8,128)(2,1)} %param.26) | copy-start | bytes 2752516
  261.7 12.0 copy-start.24
  261.7 12.0 copy-start.26
  273.7 12.0 copy-start.40
  287.1 47.0 %copy-start.11 = (f32[512,896]{1,0:T(8,128)}, f32[512,896]{1,0:T(8,128)S(1)}, u32[]{:S(2)}) copy-start(f32[512,896]{1,0:T(8,128)S(1)} %multiply_add_fusion.48) | copy-start | bytes 5505028
  291.5 8.5 copy-start.30
  300.0 7.3 copy-start.55
  308.6 92.3 %reduce-scatter.13.cloned.1.call-start = ((), (), s32[]{:S(2)}) async-start(), calls=%async_computation.16 | async-start | bytes 573440 | tf_op jit(solution)/shard_map/reduce_scatter | solution.py:286
  334.0 66.9 %reduce-scatter.17.cloned.1.call-start = ((), (), s32[]{:S(2)}) async-start(), calls=%async_computation.18 | async-start | bytes 4014080 | tf_op jit(solution)/shard_map/reduce_scatter | solution.py:288
  338.1 100.7 %reduce-scatter.11.cloned.1.call-start = ((), (), s32[]{:S(2)}) async-start(), calls=%async_computation.15 | async-start | bytes 4014080 | tf_op jit(solution)/shard_map/reduce_scatter | solution.py:285
  364.4 207.0 %reduce-scatter.23.cloned.1.call-start = ((), (), s32[]{:S(2)}) async-start(), calls=%async_computation.21 | async-start | bytes 21790720 | tf_op jit(solution)/shard_map/reduce_scatter | solution.py:291
  377.2 327.2 %reduce-scatter.21.cloned.1.call-start = ((), (), s32[]{:S(2)}) async-start(), calls=%async_computation.20 | async-start | bytes 21790720 | tf_op jit(solution)/shard_map/reduce_scatter | solution.py:290
  389.6 447.4 %reduce-scatter.19.cloned.1.call-start = ((), (), s32[]{:S(2)}) async-start(), calls=%async_computation.19 | async-start | bytes 21790720 | tf_op jit(solution)/shard_map/reduce_scatter | solution.py:289
  400.9 909.0 %all-reduce.8.cloned.1.call-start = ((), (), s32[]{:S(2)}) async-start(), calls=%async_computation.23 | async-start | bytes 29818880 | tf_op jit(solution)/shard_map/psum | solution.py:295
  836.9 472.9 %copy-start.45 = (f32[224,896]{1,0:T(8,128)S(1)}, f32[224,896]{1,0:T(8,128)}, u32[]{:S(2)}) copy-start(f32[224,896]{1,0:T(8,128)} %param.40) | copy-start | bytes 2408452
  836.9 472.9 %copy-start.46 = (f32[224,896]{1,0:T(8,128)S(1)}, f32[224,896]{1,0:T(8,128)}, u32[]{:S(2)}) copy-start(f32[224,896]{1,0:T(8,128)} %param.37) | copy-start | bytes 2408452
  1392.2 232.2 %all-to-all-start = ((f32[4,1,1290240]{2,1,0:T(1,128)}), f32[4,1,1290240]{2,1,0:T(1,128)}, u32[]{:S(2)}, u32[]{:S(2)}) async-start(f32[4,1,1290240]{2,1,0:T(1,128)} %all_to_all.26), calls=%async_computation.7 | async-start | bytes 41287680 | tf_op jit(solution)/shard_map/all_to_all | solution.py:348
  1735.9 13.3 copy-start.5
  1813.6 15.8 copy-start.15
  2460.3 13.8 copy-start.7
  2474.1 12.0 copy-start.6
  2760.1 7.3 copy-start.10
  2760.1 7.3 copy-start.19
  2760.1 7.3 copy-start.28
  2760.1 144.7 %all-to-all-start.1 = ((bf16[4,2,645120]{2,1,0:T(2,128)(2,1)}), bf16[4,2,645120]{2,1,0:T(2,128)(2,1)}, u32[]{:S(2)}, u32[]{:S(2)}) async-start(bf16[4,2,645120]{2,1,0:T(2,128)(2,1)} %reshape.355), calls=%async_computation.8 | async-start | bytes 20643840 | tf_op jit(solution)/shard_map/all_to_all | solution.py:353
  2766.4 118.0 %reduce-scatter.25.cloned.1.call-start = ((), (), s32[]{:S(2)}) async-start(), calls=%async_computation.22 | async-start | bytes 573440
  2779.0 124.6 %copy-start.69 = (f32[2,224]{1,0:T(2,128)S(1)}, f32[2,224]{1,0:T(2,128)}, u32[]{:S(2)}) copy-start(f32[2,224]{1,0:T(2,128)} %param.35) | copy-start | bytes 5380
  2779.0 124.6 %copy-start.73 = (f32[2,224]{1,0:T(2,128)S(1)}, f32[2,224]{1,0:T(2,128)}, u32[]{:S(2)}) copy-start(f32[2,224]{1,0:T(2,128)} %param.44) | copy-start | bytes 5380
  2779.0 125.2 %copy-start.71 = (f32[288]{0:T(512)S(1)}, f32[288]{0:T(512)}, u32[]{:S(2)}) copy-start(f32[288]{0:T(512)} %param.36) | copy-start | bytes 3460
  2779.0 125.2 %copy-start.74 = (f32[288]{0:T(512)S(1)}, f32[288]{0:T(512)}, u32[]{:S(2)}) copy-start(f32[288]{0:T(512)} %param.45) | copy-start | bytes 3460
  2960.8 57.5 %copy-start.52 = (f32[224,128]{1,0:T(8,128)S(1)}, f32[224,128]{1,0:T(8,128)}, u32[]{:S(2)}) copy-start(f32[224,128]{1,0:T(8,128)} %param.30) | copy-start | bytes 344068
  2960.9 58.1 %copy-start.54 = (f32[224,128]{1,0:T(8,128)S(1)}, f32[224,128]{1,0:T(8,128)}, u32[]{:S(2)}) copy-start(f32[224,128]{1,0:T(8,128)} %param.29) | copy-start | bytes 344068
  (43 other events, 159.8 us)
Sparse Core Ops, SparseCore 0:
  10.2 22.5 all-gather.6
  34.9 21.1 all-gather.8
  58.2 60.1 all-gather.12
  120.4 60.1 all-gather.10
  182.5 60.1 all-gather.14
  308.8 21.3 reduce-scatter.14
  334.1 21.3 reduce-scatter.12
  358.7 38.3 reduce-scatter.16
  400.4 38.3 reduce-scatter.10
  441.3 130.0 reduce-scatter.22
  574.2 130.0 reduce-scatter.20
  706.8 130.0 reduce-scatter.18
  843.7 466.1 all-reduce.7
  2775.7 22.7 reduce-scatter.24
where the time goes:
time: 3070 us; the launch traced here: 3060 us
  waiting for transfers between devices  1270 us (41%)
  matrix products  1110 us (36%)
  local copies, waits for them, and re-layouts  301 us (10%)
  other arithmetic  186 us (6%)
  blocking collectives  139 us (5%)
  loops' own time  30.7 us (1%)
    psum x1, waiting for transfers between devices, local(): lax.psum((part_query, part_key, part_value, part_out, part_gate, part_up,...  473 us
    dot_general x10, matrix products, orthogonal_part(): work = coef_a * work + jnp.dot(mixed, work, precision=highest)  388 us
    dot_general x10, matrix products, orthogonal_part(): square = jnp.dot(work, work.T, precision=highest)  377 us
    all_to_all x1, waiting for transfers between devices, local(): lax.all_to_all(outgoing, 'shard', split_axis=0, concat_axis=0, tiled=True)  224 us
    reduce_scatter x1, waiting for transfers between devices, local(): lax.psum_scatter(grad_up, 'shard', scatter_dimension=0, tiled=True)  133 us
    reduce_scatter x1, waiting for transfers between devices, local(): lax.psum_scatter(grad_gate, 'shard', scatter_dimension=0, tiled=True)  133 us
    reduce_scatter x1, waiting for transfers between devices, local(): lax.psum_scatter(grad_down, 'shard', scatter_dimension=0, tiled=True)  133 us
    dot_general x10, matrix products, orthogonal_part(): jnp.dot(square, square, precision=highest)  129 us
  transfers between devices with their start and end apart: 16, of which 9 were waited for; matrix products, arithmetic and copies ran while one was open for 6% of the time, Pallas kernels for 0%

commit v1 on v0

v1 whole, which is shorter than its diff:
```python
import math

import jax
import jax.numpy as jnp
from jax import lax
from jax.sharding import PartitionSpec as P

D = 896
QH = 14
KVH = 2
HD = 64
NS_ITERS = 5


eps_norm = 1e-06
theta_base = 1000000.0
coef_a = 3.4445
coef_b = -4.775
coef_c = 2.0315
momentum_decay = 0.9
muon_rate = 1.0
vector_rate = 0.1
masked_score = -1000000000.0
highest = lax.Precision.HIGHEST


def for_sending(array):

    def short(part):
        return part.astype(jnp.bfloat16) if part.dtype == jnp.float32 else part

    return jax.tree.map(short, array)


def product(left, right):
    return jnp.dot(left, right, preferred_element_type=jnp.float32)


def left_product(left, right):
    return lax.dot_general(
        left, right, (((0,), (0,)), ((), ())), preferred_element_type=jnp.float32
    )


def right_product(left, right):
    return lax.dot_general(
        left, right, (((1,), (1,)), ((), ())), preferred_element_type=jnp.float32
    )


def rope_tables(segments, head):
    length = segments.shape[-1]
    indices = jnp.arange(length, dtype=jnp.int32)
    first = jnp.ones(segments.shape[:-1] + (1,), dtype=jnp.bool_)
    change = jnp.concatenate([first, segments[..., 1:] != segments[..., :-1]], axis=-1)
    starts = lax.cummax(jnp.where(change, indices, 0), axis=segments.ndim - 1)
    place = (indices - starts).astype(jnp.float32)
    half_dim = head // 2
    inverse = jnp.exp(
        jnp.arange(half_dim, dtype=jnp.float32) * (-2.0 * math.log(theta_base) / head)
    )
    angles = place[..., None] * inverse
    angles = jnp.concatenate([angles, angles], axis=-1)
    return (jnp.cos(angles), jnp.sin(angles))


def rotary(values, cosine, sine):
    half_dim = values.shape[-1] // 2
    turned = jnp.concatenate([-values[..., half_dim:], values[..., :half_dim]], axis=-1)
    return values * cosine + turned * sine


def unrotary(grads, cosine, sine):
    half_dim = grads.shape[-1] // 2
    scaled = grads * sine
    turned = jnp.concatenate([scaled[..., half_dim:], -scaled[..., :half_dim]], axis=-1)
    return grads * cosine + turned


def norm_rows(values, gain):
    factor = lax.rsqrt(jnp.mean(values * values, axis=-1, keepdims=True) + eps_norm)
    unit = values * factor
    return (unit, factor, (unit * gain).astype(jnp.bfloat16))


def norm_back(grad_out, unit, factor, gain):
    grad_unit = grad_out * gain
    grad_gain = jnp.sum(grad_out * unit, axis=0)
    grad_in = factor * (grad_unit - unit * jnp.mean(grad_unit * unit, axis=-1, keepdims=True))
    return (grad_in, grad_gain)


def near(left, right):
    return jnp.dot(left, right, precision=lax.Precision.HIGH)


def gram_of_columns(rows):
    return lax.dot_general(
        rows, rows, (((0,), (0,)), ((), ())), precision=lax.Precision.HIGH
    )


def orthogonal_factor(gram):
    size = gram.shape[-1]
    norm = jnp.sqrt(jnp.trace(gram)) + 1e-07
    scale = 1.0 / norm
    square = gram * scale * scale
    eye = jnp.eye(size, dtype=jnp.float32)
    factor = None
    for turn in range(NS_ITERS):
        mixed = coef_b * square + coef_c * near(square, square)
        if factor is None:
            factor = coef_a * eye + mixed
        else:
            factor = coef_a * factor + near(factor, mixed)
        if turn < NS_ITERS - 1:
            half = coef_a * square + near(square, mixed)
            square = coef_a * half + near(half, mixed)
    return factor * scale


def pieces_of(rows, replicas):
    return 8 * math.ceil(rows / (8 * replicas))


def lengthened(block, rows):
    return jnp.pad(block, ((0, rows - block.shape[0]), (0, 0)))


def spread(values, group, size):
    count, width = values.shape
    parts = values.reshape(count, group, width // group)
    parts = jnp.pad(parts, ((0, 0), (0, 0), (0, size - width // group)))
    return parts.reshape(count, group * size)


def gathered_rows(array, group, rows):
    size = array.shape[0] // group
    return array.reshape(group, size, array.shape[1])[:, :rows].reshape(group * rows, array.shape[1])


def fetch(block, replica, size):
    piece = lax.dynamic_slice_in_dim(block, replica * size, size, axis=0)
    return lax.all_gather(piece, ("shard", "rep"), axis=0, tiled=True)


def total(grad):
    return lax.psum_scatter(
        grad.astype(jnp.bfloat16), ("shard", "rep"), scatter_dimension=0, tiled=True
    ).astype(jnp.float32)


def renew(momentum, grad, replica, size):
    piece = lax.dynamic_slice_in_dim(momentum, replica * size, size, axis=0)
    fresh = (momentum_decay * piece + total(grad)).astype(jnp.bfloat16)
    return lax.all_gather(fresh, ("shard", "rep"), axis=0, tiled=True)


def own_rows(array, place, group, rows):
    size = array.shape[0] // group
    return lax.dynamic_slice_in_dim(array, place * size, rows, axis=0).astype(jnp.float32)


def local(
    tokens,
    out_grad,
    segments,
    w_query,
    w_key,
    w_value,
    w_out,
    w_gate,
    w_up,
    w_down,
    gains,
    biases,
    mom_query,
    mom_key,
    mom_value,
    mom_out,
    mom_gate,
    mom_up,
    mom_down,
    gain_mom,
    bias_mom,
):
    group = lax.axis_size("shard")
    replicas = lax.axis_size("rep")
    kv_width = KVH * HD
    length = tokens.shape[0]
    place = lax.axis_index("shard")
    replica = lax.axis_index("rep")
    rows = w_gate.shape[0]
    down_rows = w_down.shape[0]
    size = pieces_of(rows, replicas)
    down_size = pieces_of(down_rows, replicas)
    tall = size * replicas
    down_tall = down_size * replicas
    attn_width = 2 * D + 2 * kv_width

    def vectors(pair, line):
        row = jnp.concatenate([pair[0], pair[1], line])
        return jnp.pad(row, (0, attn_width - row.shape[0]))[None]

    def attn_block(query, key, value, out, pair, line):
        block = jnp.concatenate([query, key, value, out], axis=1)
        return lengthened(jnp.concatenate([block, vectors(pair, line)], axis=0), tall)

    low_attn = attn_block(w_query, w_key, w_value, w_out, gains, biases).astype(jnp.bfloat16)
    low_gate = lengthened(w_gate.astype(jnp.bfloat16), tall)
    low_up = lengthened(w_up.astype(jnp.bfloat16), tall)
    low_down = lengthened(w_down.astype(jnp.bfloat16), down_tall)
    full_attn = fetch(low_attn, replica, size)
    full_gate = fetch(low_gate, replica, size)
    full_up = fetch(low_up, replica, size)
    full_down = gathered_rows(fetch(low_down, replica, down_size), group, down_rows)
    full_qkv = full_attn[:, : D + 2 * kv_width]
    full_out = full_attn[:, D + 2 * kv_width :]
    lines = full_attn.reshape(group, tall, attn_width)[:, rows]
    bias_rows = biases.shape[0]
    gain_one = lines[:, :rows].reshape(D).astype(jnp.float32)
    gain_two = lines[:, rows : 2 * rows].reshape(D).astype(jnp.float32)
    bias_all = lines[:, 2 * rows : 2 * rows + bias_rows].reshape(group * bias_rows).astype(jnp.float32)
    inputs = tokens.astype(jnp.float32)
    unit_one, factor_one, normed_one = norm_rows(inputs, gain_one)
    normed_one = spread(normed_one, group, tall)
    lin = product(normed_one, full_qkv) + bias_all
    query_lin = lin[:, :D]
    key_lin = lin[:, D : D + kv_width]
    value_lin = lin[:, D + kv_width :]
    seg_row = segments[0]
    cosine, sine = rope_tables(seg_row, HD)
    cosine = cosine[:, None, :]
    sine = sine[:, None, :]
    queries = rotary(query_lin.reshape(length, QH, HD), cosine, sine).astype(jnp.bfloat16)
    keys = rotary(key_lin.reshape(length, KVH, HD), cosine, sine).astype(jnp.bfloat16)
    values = value_lin.astype(jnp.bfloat16).reshape(length, KVH, HD)
    grouped = queries.reshape(length, KVH, QH // KVH, HD)
    score_scale = 1.0 / math.sqrt(HD)
    places = jnp.arange(length)
    allowed = (places[:, None] >= places[None, :]) & (seg_row[:, None] == seg_row[None, :])
    scores = (
        jnp.einsum("qhgd,khd->hgqk", grouped, keys, preferred_element_type=jnp.float32)
        * score_scale
    )
    probs = jax.nn.softmax(jnp.where(allowed, scores, masked_score), axis=-1)
    probs_low = probs.astype(jnp.bfloat16)
    attended = jnp.einsum("hgqk,khd->qhgd", probs_low, values, preferred_element_type=jnp.float32)
    attended = attended.reshape(length, D).astype(jnp.bfloat16)
    attended = spread(attended, group, tall)
    middle = inputs + product(attended, full_out)
    unit_two, factor_two, normed_two = norm_rows(middle, gain_two)
    normed_two = spread(normed_two, group, tall)
    gate_val = product(normed_two, full_gate)
    up_val = product(normed_two, full_up)
    sigma = jax.nn.sigmoid(gate_val)
    swish = gate_val * sigma
    hidden = (swish * up_val).astype(jnp.bfloat16)
    result = (middle + product(hidden, full_down)).astype(jnp.bfloat16)

    def narrowed(values):
        return values.reshape(length, group, tall)[:, :, :rows].reshape(length, D)

    cotangent = out_grad.astype(jnp.float32)
    grad_down = left_product(hidden, out_grad)
    dhidden = right_product(out_grad, full_down)
    dgate = (dhidden * up_val * sigma * (1.0 + gate_val * (1.0 - sigma))).astype(jnp.bfloat16)
    dup = (dhidden * swish).astype(jnp.bfloat16)
    grad_gate = left_product(normed_two, dgate)
    grad_up = left_product(normed_two, dup)
    dnormed_two = right_product(dgate, full_gate) + right_product(dup, full_up)
    dnormed_two = narrowed(dnormed_two)
    dmiddle_norm, grad_gain_two = norm_back(dnormed_two, unit_two, factor_two, gain_two)
    dmiddle = cotangent + dmiddle_norm
    dmid_low = dmiddle.astype(jnp.bfloat16)
    grad_out = left_product(attended, dmid_low)
    dattended = (
        narrowed(right_product(dmid_low, full_out)).astype(jnp.bfloat16).reshape(length, KVH, QH // KVH, HD)
    )
    dvalues = jnp.einsum("hgqk,qhgd->khd", probs_low, dattended, preferred_element_type=jnp.float32)
    dvalues = dvalues.reshape(length, kv_width).astype(jnp.bfloat16)
    dprobs = jnp.einsum("qhgd,khd->hgqk", dattended, values, preferred_element_type=jnp.float32)
    dscores = (
        probs * (dprobs - jnp.sum(probs * dprobs, axis=-1, keepdims=True)) * score_scale
    ).astype(jnp.bfloat16)
    dquery = jnp.einsum(
        "hgqk,khd->qhgd", dscores, keys, preferred_element_type=jnp.float32
    ).reshape(length, QH, HD)
    dkey = jnp.einsum("hgqk,qhgd->khd", dscores, grouped, preferred_element_type=jnp.float32)
    dquery = unrotary(dquery, cosine, sine).reshape(length, D).astype(jnp.bfloat16)
    dkey = unrotary(dkey, cosine, sine).reshape(length, kv_width).astype(jnp.bfloat16)
    dqkv = jnp.concatenate([dquery, dkey, dvalues], axis=1)
    grad_qkv = left_product(normed_one, dqkv)
    grad_biases = jnp.sum(dqkv.astype(jnp.float32), axis=0)
    dnormed_one = narrowed(right_product(dqkv, full_qkv))
    dinput_norm, grad_gain_one = norm_back(dnormed_one, unit_one, factor_one, gain_one)
    input_grad = dmiddle + dinput_norm
    grad_attn = jnp.concatenate([grad_qkv, grad_out], axis=1)
    grad_lines = jnp.concatenate(
        [
            grad_gain_one.reshape(group, rows),
            grad_gain_two.reshape(group, rows),
            grad_biases.reshape(group, bias_rows),
        ],
        axis=1,
    )
    grad_lines = jnp.pad(grad_lines, ((0, 0), (0, attn_width - 2 * rows - bias_rows)))
    grad_attn = grad_attn.reshape(group, tall, attn_width)
    grad_attn = jnp.concatenate(
        [grad_attn[:, :rows], grad_lines[:, None], grad_attn[:, rows + 1 :]], axis=1
    ).reshape(group * tall, attn_width)
    grad_down = jnp.pad(
        grad_down.astype(jnp.bfloat16).reshape(group, down_rows, D),
        ((0, 0), (0, down_tall - down_rows), (0, 0)),
    ).reshape(group * down_tall, D)
    mom_attn = attn_block(mom_query, mom_key, mom_value, mom_out, gain_mom, bias_mom)
    whole_down = renew(lengthened(mom_down, down_tall), grad_down, replica, down_size)
    whole_gate = renew(lengthened(mom_gate, tall), grad_gate, replica, size)
    whole_up = renew(lengthened(mom_up, tall), grad_up, replica, size)
    whole_attn = renew(mom_attn, grad_attn, replica, size)
    new_gate = own_rows(whole_gate, place, group, rows)
    new_up = own_rows(whole_up, place, group, rows)
    new_down = own_rows(whole_down, place, group, down_rows)
    new_attn = own_rows(whole_attn, place, group, rows)
    new_line = lax.dynamic_slice_in_dim(whole_attn, place * tall + rows, 1, axis=0)[0].astype(jnp.float32)
    new_query = new_attn[:, :D]
    new_key = new_attn[:, D : D + kv_width]
    new_value = new_attn[:, D + kv_width : D + 2 * kv_width]
    new_out = new_attn[:, D + 2 * kv_width :]
    token_total = length * group * replicas
    gain_mom_new = new_line[: 2 * rows].reshape(2, rows)
    gains_new = gains - vector_rate * gain_mom_new / math.sqrt(token_total)
    bias_mom_new = new_line[2 * rows : 2 * rows + bias_rows]
    biases_new = biases - vector_rate * bias_mom_new / math.sqrt(token_total)
    odd = replica % 2 == 1
    flat_attn = gathered_rows(whole_attn, group, rows)
    square_query = flat_attn[:, :D]
    square_out = flat_attn[:, D + 2 * kv_width :]

    def row_gram(whole):
        gram = right_product(whole, whole).reshape(group, tall, group, tall)
        return gram[:, :rows, :, :rows].reshape(D, D)

    def column_gram(whole):
        return left_product(whole, whole)

    gram = lax.switch(
        jnp.minimum(place, 3),
        [
            lambda: row_gram(whole_gate),
            lambda: row_gram(whole_up),
            lambda: column_gram(whole_down),
            lambda: column_gram(jnp.where(odd, square_out, square_query)),
        ],
    )
    factor = orthogonal_factor(gram).astype(jnp.bfloat16)
    factors = lax.all_gather(factor, "shard", axis=0, tiled=False)
    pairs = [(item, item ^ 1) for item in range(replicas)]
    other = lax.ppermute(factors[3], "rep", pairs)
    factor_query = jnp.where(odd, other, factors[3])
    factor_out = jnp.where(odd, factors[3], other)
    wide = math.sqrt(w_gate.shape[1] / D)

    def slab(item):
        block = lax.dynamic_slice_in_dim(factors[item], place * rows, rows, axis=0)
        return spread(block, group, tall)

    step_gate = wide * product(slab(0), whole_gate)
    step_up = wide * product(slab(1), whole_up)
    step_down = product(new_down.astype(jnp.bfloat16), factors[2])
    step_query = product(new_query.astype(jnp.bfloat16), factor_query)
    step_out = product(new_out.astype(jnp.bfloat16), factor_out)
    step_key = near(new_key, orthogonal_factor(column_gram(flat_attn[:, D : D + kv_width])))
    step_value = near(
        new_value, orthogonal_factor(column_gram(flat_attn[:, D + kv_width : D + 2 * kv_width]))
    )
    upd_gate = w_gate - muon_rate * step_gate
    upd_up = w_up - muon_rate * step_up
    upd_down = w_down - muon_rate * step_down
    upd_query = w_query - muon_rate * step_query
    upd_out = w_out - muon_rate * step_out
    upd_key = w_key - muon_rate * step_key
    upd_value = w_value - muon_rate * step_value
    return (
        result,
        input_grad,
        new_query,
        new_key,
        new_value,
        new_out,
        new_gate,
        new_up,
        new_down,
        upd_query,
        upd_key,
        upd_value,
        upd_out,
        upd_gate,
        upd_up,
        upd_down,
        gain_mom_new,
        gains_new,
        bias_mom_new,
        biases_new,
    )


def solution(mesh):
    placed = (
        P(("shard", "rep"), None),
        P(("shard", "rep"), None),
        P(("shard", "rep"), None),
        P("shard", None),
        P("shard", None),
        P("shard", None),
        P("shard", None),
        P("shard", None),
        P("shard", None),
        P("shard", None),
        P(None, "shard"),
        P("shard"),
        P("shard", None),
        P("shard", None),
        P("shard", None),
        P("shard", None),
        P("shard", None),
        P("shard", None),
        P("shard", None),
        P(None, "shard"),
        P("shard"),
    )
    return jax.shard_map(
        local,
        mesh=mesh,
        in_specs=placed,
        out_specs=(
            P(("shard", "rep"), None),
            P(("shard", "rep"), None),
            P("shard", None),
            P("shard", None),
            P("shard", None),
            P("shard", None),
            P("shard", None),
            P("shard", None),
            P("shard", None),
            P("shard", None),
            P("shard", None),
            P("shard", None),
            P("shard", None),
            P("shard", None),
            P("shard", None),
            P("shard", None),
            P(None, "shard"),
            P(None, "shard"),
            P("shard"),
            P("shard"),
        ),
        check_vma=False,
    )
```

time: 3070 us -> 1820 us (0.59)
  matrix products: 1110 us -> 356 us
  local copies, waits for them, and re-layouts: 301 us -> 67.4 us
  blocking collectives: 139 us -> 0 us
  other arithmetic: 186 us -> 57 us
    dot_general x30 -> x53, matrix products: 894 us -> 115 us  [near(): return jnp.dot(left, right, precision=lax.Precision.HIGH)]
    psum x1 -> x0, waiting for transfers between devices: 473 us -> none  [local(): lax.psum((part_query, part_key, part_value, part_out, part_gate, part_up,...]
    all_gather x5 -> x9, waiting for transfers between devices: 134 us -> 560 us  [the longest x4 291 us: renew(): return lax.all_gather(fresh, ('shard', 'rep'), axis=0, tiled=True)]
    all_to_all x2 -> x0, waiting for transfers between devices: 224 us -> none  [the longest x1 224 us: local(): lax.all_to_all(outgoing, 'shard', split_axis=0, concat_axis=0, tiled=True)]
    unnamed x15 -> x14, waiting for transfers between devices: 0.23 us -> 198 us
    reduce_scatter x7 -> x3, waiting for transfers between devices: 436 us -> 543 us  [total(): lax.psum_scatter(grad.astype(jnp.bfloat16), ('shard', 'rep'), scatter_dim...]
    unnamed x2 -> x0, blocking collectives: 102 us -> none
    unnamed x151 -> x96, local copies, waits for them, and re-layouts: 105 us -> 6.6 us
  transfers between devices with their start and end apart: 16 -> 14, of which waited for: 9 -> 14; matrix products, arithmetic and copies ran while one was open for 6% -> 11% of each run, Pallas kernels for 0% -> 0%
where the time goes in v1:
time: 1820 us; the launch traced here: 1810 us
  waiting for transfers between devices  1300 us (71%)
  matrix products  356 us (20%)
  local copies, waits for them, and re-layouts  67.4 us (4%)
  other arithmetic  57 us (3%)
    reduce_scatter x3, waiting for transfers between devices, total(): lax.psum_scatter(grad.astype(jnp.bfloat16), ('shard', 'rep'), scatter_dim...  543 us
    all_gather x4, waiting for transfers between devices, renew(): return lax.all_gather(fresh, ('shard', 'rep'), axis=0, tiled=True)  291 us
    all_gather x4, waiting for transfers between devices, fetch(): return lax.all_gather(piece, ('shard', 'rep'), axis=0, tiled=True)  248 us
    unnamed x14, waiting for transfers between devices  198 us
    dot_general x53, matrix products, near(): return jnp.dot(left, right, precision=lax.Precision.HIGH)  115 us
    dot_general x10, matrix products, product(): return jnp.dot(left, right, preferred_element_type=jnp.float32)  70.4 us
    dot_general x5, matrix products, right_product(): lax.dot_general(left, right, (((1,), (1,)), ((), ())), preferred_element_...  56.7 us
    dot_general x7, matrix products, left_product(): lax.dot_general(left, right, (((0,), (0,)), ((), ())), preferred_element_...  37.7 us
  transfers between devices with their start and end apart: 14, of which 14 were waited for; matrix products, arithmetic and copies ran while one was open for 11% of the time, Pallas kernels for 0%

profile of v1, /device:TPU:0, one launch (start us, length us, event | category | flops | bytes accessed | tf_op | source)
XLA Modules:
  0.0 1812.0 jit_solution(13340212328475147424)
XLA Ops:
  24.8 54.1 %all-gather.11.cloned.1.call-done = bf16[1024,2048]{1,0:T(8,128)(2,1)} async-done(((bf16[32,2048]{1,0:T(8,128)(2,1)}), bf16[1024,2048]{1,0:T(8,128)(2,1)}) %all-gather.11.cloned.1.call-update) | async-done | bytes 4194320 | tf_op jit(solution)/shard_map/all_gather | solution.py:144
  90.0 11.5 fusion.266
  101.5 6.6 fusion.126
  115.2 50.0 %all-gather.13.cloned.1.call-done = bf16[1024,4864]{1,0:T(8,128)(2,1)} async-done(((bf16[32,4864]{1,0:T(8,128)(2,1)}), bf16[1024,4864]{1,0:T(8,128)(2,1)}) %all-gather.13.cloned.1.call-update) | async-done | bytes 9961488 | tf_op jit(solution)/shard_map/all_gather | solution.py:144
  165.2 11.8 fusion.270
  177.0 74.5 %all-gather.15.cloned.1.call-done = bf16[1024,4864]{1,0:T(8,128)(2,1)} async-done(((bf16[32,4864]{1,0:T(8,128)(2,1)}), bf16[1024,4864]{1,0:T(8,128)(2,1)}) %all-gather.15.cloned.1.call-update) | async-done | bytes 9961488 | tf_op jit(solution)/shard_map/all_gather | solution.py:144
  251.6 11.7 fusion.271
  263.2 69.0 %all-gather.17.cloned.1.call-done = bf16[4864,896]{1,0:T(8,128)(2,1)} async-done(((bf16[152,896]{1,0:T(8,128)(2,1)}), bf16[4864,896]{1,0:T(8,128)(2,1)}) %all-gather.17.cloned.1.call-update) | async-done | bytes 8716304 | tf_op jit(solution)/shard_map/all_gather | solution.py:144
  332.3 17.4 fusion.14
  349.7 9.6 fusion.272
  359.3 8.2 convolution_add_fusion.1
  387.5 8.5 fusion.139
  396.1 7.2 fusion.273
  403.3 19.3 %broadcast_multiply_fusion = (f32[512,2,64]{0,2,1:T(8,128)S(1)}, f32[512,2,64]{0,2,1:T(8,128)S(1)}) fusion(f32[512,64]{0,1:T(8,128)S(1)} %get-tuple-element.62, bf16[512,2,7,64]{0,3,2,1:T(8,128)(2,1)S(1)} %copy-done.20, f32[2,512,512,7]{2,1,3,0:T(8,128)} %fusion.273, f32[2,7,512,512]{2,3,1,0:T(8,128)} %get-tuple-element.68, f32[2,7,512]{2,1,0:T(8,128)S(1)} %copy-done.41), kind=kOutput, calls=%fused_computation.297 | convolution fusion | flops 495525376 | bytes 30961664 | tf_op jit(solution)/shard_map/hgqk,qhgd->khd/dot_general | solution.py:289
  422.6 21.0 %fusion.23 = f32[2,64,7,512]{3,1,2,0:T(8,128)} fusion(bf16[512,2,64,1]{0,2,3,1:T(8,128)(2,1)} %copy-done.25, f32[2,512,512,7]{2,1,3,0:T(8,128)} %fusion.273, f32[2,7,512,512]{2,3,1,0:T(8,128)} %get-tuple-element.68, f32[2,7,512]{2,1,0:T(8,128)} %copy-done.39), kind=kOutput, calls=%fused_computation.38 | convolution fusion | flops 495459840 | bytes 31354880 | tf_op jit(solution)/shard_map/hgqk,khd->qhgd/dot_general | solution.py:286
  467.9 9.6 convolution_convert_fusion.2
  477.6 10.4 convolution_convert_fusion.1
  488.0 10.6 convolution_convert_fusion
  500.8 109.7 %reduce-scatter.8.cloned.1.call-done = bf16[32,2048]{1,0:T(8,128)(2,1)} async-done(((bf16[1024,2048]{1,0:T(8,128)(2,1)}), bf16[32,2048]{1,0:T(8,128)(2,1)}) %reduce-scatter.8.cloned.1.call-update) | async-done | bytes 131088 | tf_op jit(solution)/shard_map/reduce_scatter | solution.py:148
  612.5 198.2 %reduce-scatter.14.cloned.1.call-done = bf16[152,896]{1,0:T(8,128)(2,1)} async-done(((bf16[4864,896]{1,0:T(8,128)(2,1)}), bf16[152,896]{1,0:T(8,128)(2,1)}) %reduce-scatter.14.cloned.1.call-update) | async-done | bytes 272400
  812.7 217.1 %reduce-scatter.10.cloned.1.call-done = bf16[32,4864]{1,0:T(8,128)(2,1)} async-done(((bf16[1024,4864]{1,0:T(8,128)(2,1)}), bf16[32,4864]{1,0:T(8,128)(2,1)}) %reduce-scatter.10.cloned.1.call-update) | async-done | bytes 311312 | tf_op jit(solution)/shard_map/reduce_scatter | solution.py:148
  1031.8 216.0 %reduce-scatter.12.cloned.1.call-done = bf16[32,4864]{1,0:T(8,128)(2,1)} async-done(((bf16[1024,4864]{1,0:T(8,128)(2,1)}), bf16[32,4864]{1,0:T(8,128)(2,1)}) %reduce-scatter.12.cloned.1.call-update) | async-done | bytes 311312 | tf_op jit(solution)/shard_map/reduce_scatter | solution.py:148
  1253.6 10.5 add_convert_fusion
  1264.2 48.7 %all-gather.19.cloned.1.call-done = bf16[1024,2048]{1,0:T(8,128)(2,1)} async-done(((bf16[32,2048]{1,0:T(8,128)(2,1)}), bf16[1024,2048]{1,0:T(8,128)(2,1)}) %all-gather.19.cloned.1.call-update) | async-done | bytes 4194320 | tf_op jit(solution)/shard_map/all_gather | solution.py:156
  1324.1 69.3 %all-gather.25.cloned.1.call-done = bf16[4864,896]{1,0:T(8,128)(2,1)} async-done(((bf16[152,896]{1,0:T(8,128)(2,1)}), bf16[4864,896]{1,0:T(8,128)(2,1)}) %all-gather.25.cloned.1.call-update) | async-done | bytes 8716304 | tf_op jit(solution)/shard_map/all_gather | solution.py:156
  1393.4 86.4 %all-gather.21.cloned.1.call-done = bf16[1024,4864]{1,0:T(8,128)(2,1)} async-done(((bf16[32,4864]{1,0:T(8,128)(2,1)}), bf16[1024,4864]{1,0:T(8,128)(2,1)}) %all-gather.21.cloned.1.call-update) | async-done | bytes 9961488 | tf_op jit(solution)/shard_map/all_gather | solution.py:156
  1479.8 86.2 %all-gather.23.cloned.1.call-done = bf16[1024,4864]{1,0:T(8,128)(2,1)} async-done(((bf16[32,4864]{1,0:T(8,128)(2,1)}), bf16[1024,4864]{1,0:T(8,128)(2,1)}) %all-gather.23.cloned.1.call-update) | async-done | bytes 9961488 | tf_op jit(solution)/shard_map/all_gather | solution.py:156
  1566.0 40.9 %conditional.1 = (f32[896,896]{1,0:T(8,128)S(1)}) conditional(s32[]{:T(128)} %clamp.3, bf16[1024,4864]{1,0:T(8,128)(2,1)} %all-gather.21.cloned.1.call-done, bf16[1024,4864]{1,0:T(8,128)(2,1)} %all-gather.23.cloned.1.call-done, bf16[4864,896]{1,0:T(8,128)(2,1)} %all-gather.25.cloned.1.call-done, (pred[]{:T(512)}, ...), branch_computations={%region_16.17_spmd, %region_17.18_spmd, %region_18.19_spmd, %regio... | conditional | flops 10200547328 | bytes 35389448 | solution.py:347
  1566.0 17.7 fusion.267
  1614.2 6.1 multiply_add_fusion.21
  1620.3 6.2 multiply_add_fusion.20
  1632.5 7.0 multiply_add_fusion.22
  1639.5 6.0 multiply_add_fusion.14
  1645.5 6.3 multiply_add_fusion.13
  1651.8 5.9 fusion.275
  1657.7 6.2 multiply_add_fusion.7
  1664.0 6.0 multiply_add_fusion.15
  1670.0 6.4 multiply_add_fusion.6
  1676.4 5.9 fusion.276
  1682.4 6.2 multiply_add_fusion.1
  1688.6 6.0 multiply_add_fusion.8
  1694.6 6.4 multiply_add_fusion
  1701.0 5.9 fusion.277
  1707.0 7.5 multiply_convert_fusion.1
  1738.5 22.1 %all-gather.27.cloned.1.call-done = bf16[3584,896]{1,0:T(8,128)(2,1)} async-done(((bf16[896,896]{1,0:T(8,128)(2,1)}), bf16[3584,896]{1,0:T(8,128)(2,1)}) %all-gather.27.cloned.1.call-update) | async-done | bytes 6422544 | tf_op jit(solution)/shard_map/all_gather | solution.py:357
  1770.4 9.6 fusion.20
  1783.5 8.3 convolution_subtract_fusion
  1791.8 8.4 fusion.21
  (283 shorter events, 172.1 us)
Async XLA Ops:
  7.2 71.7 %all-gather.11.cloned.1.call-start = ((), (), s32[]{:S(2)}) async-start(), calls=%async_computation.4 | async-start | bytes 4325376 | tf_op jit(solution)/shard_map/all_gather | solution.py:144
  13.9 151.3 %all-gather.13.cloned.1.call-start = ((), (), s32[]{:S(2)}) async-start(), calls=%async_computation.5 | async-start | bytes 10272768 | tf_op jit(solution)/shard_map/all_gather | solution.py:144
  17.2 234.3 %all-gather.15.cloned.1.call-start = ((), (), s32[]{:S(2)}) async-start(), calls=%async_computation.6 | async-start | bytes 10272768 | tf_op jit(solution)/shard_map/all_gather | solution.py:144
  19.7 3.9 copy-start.1
  20.6 311.7 %all-gather.17.cloned.1.call-start = ((), (), s32[]{:S(2)}) async-start(), calls=%async_computation.7 | async-start | bytes 8988672 | tf_op jit(solution)/shard_map/all_gather | solution.py:144
  22.4 588.1 %reduce-scatter.8.cloned.1.call-start = ((), (), s32[]{:S(2)}) async-start(), calls=%async_computation.8 | async-start | bytes 4325376 | tf_op jit(solution)/shard_map/reduce_scatter | solution.py:148
  23.6 65.0 %copy-start.11 = (f32[512,64]{0,1:T(8,128)}, f32[512,64]{0,1:T(8,128)S(1)}, u32[]{:S(2)}) copy-start(f32[512,64]{0,1:T(8,128)S(1)} %get-tuple-element.61) | copy-start | bytes 393220
  23.9 57.2 %copy-start.31 = (f32[512]{0:T(512)}, f32[512]{0:T(512)S(1)}, u32[]{:S(2)}) copy-start(f32[512]{0:T(512)S(1)} %add_rsqrt_fusion.1) | copy-start | bytes 6148
  81.1 3.7 copy-start.7
  101.5 6.6 copy-start.39
  115.2 136.3 %copy-start.4 = (bf16[512,4,256]{0,2,1:T(8,128)(2,1)}, bf16[512,4,256]{0,2,1:T(8,128)(2,1)S(1)}, u32[]{:S(2)}) copy-start(bf16[512,4,256]{0,2,1:T(8,128)(2,1)S(1)} %pad.56) | copy-start | bytes 3145732
  349.7 9.6 copy-start.3
  373.7 5.0 copy-start.19
  387.5 8.5 copy-start.10
  396.1 7.2 copy-start.20
  396.1 7.2 copy-start.41
  422.6 21.1 %copy-start.18 = (bf16[512,4,256]{0,2,1:T(8,128)(2,1)S(1)}, bf16[512,4,256]{0,2,1:T(8,128)(2,1)}, u32[]{:S(2)}) copy-start(bf16[512,4,256]{0,2,1:T(8,128)(2,1)} %pad.55) | copy-start | bytes 3145732
  451.5 3.5 copy-start.17
  456.6 4.1 copy-start.2
  456.6 4.1 copy-start.28
  456.6 4.1 copy-start.32
  467.8 342.8 %reduce-scatter.14.cloned.1.call-start = ((), (), s32[]{:S(2)}) async-start(), calls=%async_computation.16 | async-start | bytes 8988672
  477.5 552.3 %reduce-scatter.10.cloned.1.call-start = ((), (), s32[]{:S(2)}) async-start(), calls=%async_computation.10 | async-start | bytes 10272768 | tf_op jit(solution)/shard_map/reduce_scatter | solution.py:148
  488.0 759.8 %reduce-scatter.12.cloned.1.call-start = ((), (), s32[]{:S(2)}) async-start(), calls=%async_computation.12 | async-start | bytes 10272768 | tf_op jit(solution)/shard_map/reduce_scatter | solution.py:148
  498.6 111.9 %copy-start.21 = (f32[224,896]{1,0:T(8,128)S(1)}, f32[224,896]{1,0:T(8,128)}, u32[]{:S(2)}) copy-start(f32[224,896]{1,0:T(8,128)} %param.40) | copy-start | bytes 2408452
  498.6 814.2 %all-gather.19.cloned.1.call-start = ((), (), s32[]{:S(2)}) async-start(), calls=%async_computation.9 | async-start | bytes 4325376 | tf_op jit(solution)/shard_map/all_gather | solution.py:156
  612.4 781.0 %all-gather.25.cloned.1.call-start = ((), (), s32[]{:S(2)}) async-start(), calls=%async_computation.14 | async-start | bytes 8988672 | tf_op jit(solution)/shard_map/all_gather | solution.py:156
  812.6 667.2 %all-gather.21.cloned.1.call-start = ((), (), s32[]{:S(2)}) async-start(), calls=%async_computation.11 | async-start | bytes 10272768 | tf_op jit(solution)/shard_map/all_gather | solution.py:156
  1031.7 218.1 %copy-start.34 = (f32[512]{0:T(512)S(1)}, f32[512]{0:T(512)}, u32[]{:S(2)}) copy-start(f32[512]{0:T(512)} %get-tuple-element.40) | copy-start | bytes 6148
  1031.7 218.1 %copy-start.29 = (f32[896]{0:T(1024)S(1)}, f32[896]{0:T(1024)}, u32[]{:S(2)}) copy-start(f32[896]{0:T(1024)} %copy-done.27) | copy-start | bytes 10756
  1031.7 218.1 %copy-start.33 = (f32[512]{0:T(512)S(1)}, f32[512]{0:T(512)}, u32[]{:S(2)}) copy-start(f32[512]{0:T(512)} %copy-done.31) | copy-start | bytes 6148
  1031.8 534.3 %all-gather.23.cloned.1.call-start = ((), (), s32[]{:S(2)}) async-start(), calls=%async_computation.13 | async-start | bytes 10272768 | tf_op jit(solution)/shard_map/all_gather | solution.py:156
  1249.8 510.8 %all-gather.27.cloned.1.call-start = ((), (), s32[]{:S(2)}) async-start(), calls=%async_computation.15 | async-start | bytes 8028160 | tf_op jit(solution)/shard_map/all_gather | solution.py:357
  1312.8 9.6 copy-start.36
  1322.3 243.7 %copy-start.38 = (f32[2,224]{1,0:T(2,128)}, f32[2,224]{1,0:T(2,128)S(1)}, u32[]{:S(2)}) copy-start(f32[2,224]{1,0:T(2,128)S(1)} %reshape.337) | copy-start | bytes 5380
  1322.4 392.1 %copy-start.35 = (f32[288]{0:T(512)}, f32[288]{0:T(512)S(1)}, u32[]{:S(2)}) copy-start(f32[288]{0:T(512)S(1)} %slice_reduce_fusion.2) | copy-start | bytes 3460
  1707.0 7.6 copy-start.37
  1714.5 5.8 copy-start.22
  1714.6 7.4 copy-start.23
  1726.0 76.0 %copy-start.16 = (f32[224,896]{1,0:T(8,128)}, f32[224,896]{1,0:T(8,128)S(1)}, u32[]{:S(2)}) copy-start(f32[224,896]{1,0:T(8,128)S(1)} %get-tuple-element.50) | copy-start | bytes 2408452
  1726.0 77.6 %copy-start.15 = (f32[224,896]{1,0:T(8,128)}, f32[224,896]{1,0:T(8,128)S(1)}, u32[]{:S(2)}) copy-start(f32[224,896]{1,0:T(8,128)S(1)} %get-tuple-element.49) | copy-start | bytes 2408452
  1764.5 37.5 %collective-permute-start = (bf16[896,896]{1,0:T(8,128)(2,1)}, bf16[896,896]{1,0:T(8,128)(2,1)S(1)}, u32[]{:S(2)}, u32[]{:S(2)}) collective-permute-start(bf16[896,896]{1,0:T(8,128)(2,1)} %get-tuple-element.48), channel_id=1, source_target_pairs={{0,1},{1,0},{2,3},{3,2},{4,5},{5,4},{6,7},{7,6},{8,9},{9,8},{10,11... | collective-permute-start | bytes 4816904 | tf_op jit(solution)/shard_map/ppermute | solution.py:359
  1770.4 21.4 %slice-start = ((s8[4358144]{0:T(1024)(128)(4,1)}), s8[163840]{0:T(1024)(128)(4,1)S(1)}, s32[]{:S(2)}) async-start(s8[4358144]{0:T(1024)(128)(4,1)} %bitcast.257), calls=%async_computation.17 | async-start | bytes 327680
  1783.4 18.6 %slice-start.2 = ((s8[6422528]{0:T(1024)(128)(4,1)}), s8[4194304]{0:T(1024)(128)(4,1)S(1)}, s32[]{:S(2)}) async-start(s8[6422528]{0:T(1024)(128)(4,1)} %bitcast.264), calls=%async_computation.19 | async-start | bytes 8388608
  1783.5 8.3 slice-start.1
  1783.5 18.5 %slice-start.3 = ((s8[6422528]{0:T(1024)(128)(4,1)}), s8[2228224]{0:T(1024)(128)(4,1)S(1)}, s32[]{:S(2)}) async-start(s8[6422528]{0:T(1024)(128)(4,1)} %bitcast.264), calls=%async_computation.20 | async-start | bytes 4456448
  1791.8 10.2 copy-start.13
  1800.2 3.4 copy-start.14
  (12 other events, 21.6 us)
Sparse Core Ops, SparseCore 0:
  14.0 64.8 all-gather.10
  82.3 82.8 all-gather.12
  168.6 82.8 all-gather.14
  254.8 77.4 all-gather.16
  468.0 142.5 reduce-scatter.7
  612.7 197.9 reduce-scatter.13
  813.0 216.7 reduce-scatter.9
  1032.2 215.5 reduce-scatter.11
  1251.4 61.4 all-gather.18
  1316.1 77.2 all-gather.24
  1396.9 82.9 all-gather.20
  1483.1 82.8 all-gather.22
  1714.7 45.8 all-gather.26

commit v2 on v1

--- a/solution.py
+++ b/solution.py
@@ -139,20 +139,25 @@
     return array.reshape(group, size, array.shape[1])[:, :rows].reshape(group * rows, array.shape[1])
 
 
-def fetch(block, replica, size):
-    piece = lax.dynamic_slice_in_dim(block, replica * size, size, axis=0)
-    return lax.all_gather(piece, ("shard", "rep"), axis=0, tiled=True)
-
-
-def total(grad):
+def fetch(block):
+    return lax.all_gather(block, "shard", axis=0, tiled=True)
+
+
+def group_total(grad):
     return lax.psum_scatter(
-        grad.astype(jnp.bfloat16), ("shard", "rep"), scatter_dimension=0, tiled=True
-    ).astype(jnp.float32)
-
-
-def renew(momentum, grad, replica, size):
+        grad.astype(jnp.bfloat16), "shard", scatter_dimension=0, tiled=True
+    )
+
+
+def total(part, rows):
+    return lax.psum_scatter(
+        lengthened(part, rows), "rep", scatter_dimension=0, tiled=True
+    )
+
+
+def renew(momentum, summed, replica, size):
     piece = lax.dynamic_slice_in_dim(momentum, replica * size, size, axis=0)
-    fresh = (momentum_decay * piece + total(grad)).astype(jnp.bfloat16)
+    fresh = (momentum_decay * piece + summed.astype(jnp.float32)).astype(jnp.bfloat16)
     return lax.all_gather(fresh, ("shard", "rep"), axis=0, tiled=True)
 
 
@@ -207,13 +212,10 @@
         return lengthened(jnp.concatenate([block, vectors(pair, line)], axis=0), tall)
 
     low_attn = attn_block(w_query, w_key, w_value, w_out, gains, biases).astype(jnp.bfloat16)
-    low_gate = lengthened(w_gate.astype(jnp.bfloat16), tall)
-    low_up = lengthened(w_up.astype(jnp.bfloat16), tall)
-    low_down = lengthened(w_down.astype(jnp.bfloat16), down_tall)
-    full_attn = fetch(low_attn, replica, size)
-    full_gate = fetch(low_gate, replica, size)
-    full_up = fetch(low_up, replica, size)
-    full_down = gathered_rows(fetch(low_down, replica, down_size), group, down_rows)
+    full_attn = fetch(low_attn)
+    full_gate = fetch(w_gate.astype(jnp.bfloat16))
+    full_up = fetch(w_up.astype(jnp.bfloat16))
+    full_down = fetch(w_down.astype(jnp.bfloat16))
     full_qkv = full_attn[:, : D + 2 * kv_width]
     full_out = full_attn[:, D + 2 * kv_width :]
     lines = full_attn.reshape(group, tall, attn_width)[:, rows]
@@ -250,7 +252,6 @@
     attended = spread(attended, group, tall)
     middle = inputs + product(attended, full_out)
     unit_two, factor_two, normed_two = norm_rows(middle, gain_two)
-    normed_two = spread(normed_two, group, tall)
     gate_val = product(normed_two, full_gate)
     up_val = product(normed_two, full_up)
     sigma = jax.nn.sigmoid(gate_val)
@@ -269,7 +270,10 @@
     grad_gate = left_product(normed_two, dgate)
     grad_up = left_product(normed_two, dup)
     dnormed_two = right_product(dgate, full_gate) + right_product(dup, full_up)
-    dnormed_two = narrowed(dnormed_two)
+    grad_down, grad_gate, grad_up = for_sending((grad_down, grad_gate, grad_up))
+    grad_down, grad_gate, grad_up, dnormed_two = lax.optimization_barrier(
+        (grad_down, grad_gate, grad_up, dnormed_two)
+    )
     dmiddle_norm, grad_gain_two = norm_back(dnormed_two, unit_two, factor_two, gain_two)
     dmiddle = cotangent + dmiddle_norm
     dmid_low = dmiddle.astype(jnp.bfloat16)
@@ -309,15 +313,24 @@
     grad_attn = jnp.concatenate(
         [grad_attn[:, :rows], grad_lines[:, None], grad_attn[:, rows + 1 :]], axis=1
     ).reshape(group * tall, attn_width)
-    grad_down = jnp.pad(
-        grad_down.astype(jnp.bfloat16).reshape(group, down_rows, D),
-        ((0, 0), (0, down_tall - down_rows), (0, 0)),
-    ).reshape(group * down_tall, D)
+    part_down = group_total(grad_down)
+    part_gate = group_total(grad_gate)
+    part_up = group_total(grad_up)
+    grad_attn = lax.optimization_barrier(
+        (grad_attn.astype(jnp.bfloat16), part_down, part_gate, part_up)
+    )[0]
+    part_attn = group_total(grad_attn)
+    sum_down = total(part_down, down_tall)
+    sum_gate = total(part_gate, tall)
+    sum_up = total(part_up, tall)
+    sum_attn = total(part_attn, tall)
     mom_attn = attn_block(mom_query, mom_key, mom_value, mom_out, gain_mom, bias_mom)
-    whole_down = renew(lengthened(mom_down, down_tall), grad_down, replica, down_size)
-    whole_gate = renew(lengthened(mom_gate, tall), grad_gate, replica, size)
-    whole_up = renew(lengthened(mom_up, tall), grad_up, replica, size)
-    whole_attn = renew(mom_attn, grad_attn, replica, size)
+    whole_down = gathered_rows(
+        renew(lengthened(mom_down, down_tall), sum_down, replica, down_size), group, down_rows
+    )
+    whole_gate = renew(lengthened(mom_gate, tall), sum_gate, replica, size)
+    whole_up = renew(lengthened(mom_up, tall), sum_up, replica, size)
+    whole_attn = renew(mom_attn, sum_attn, replica, size)
     new_gate = own_rows(whole_gate, place, group, rows)
     new_up = own_rows(whole_up, place, group, rows)
     new_down = own_rows(whole_down, place, group, down_rows)

time: 1820 us -> 1450 us (0.80)
  waiting for transfers between devices: 1300 us -> 917 us
    reduce_scatter x3 -> x7, waiting for transfers between devices: 543 us -> 373 us  [the longest x3 200 us: total(): lax.psum_scatter(lengthened(part, rows), 'rep', scatter_dimension=0, tile...]
    unnamed x14 -> x18, waiting for transfers between devices: 198 us -> 77.1 us
    all_gather x4, waiting for transfers between devices: 248 us -> 151 us  [fetch(): return lax.all_gather(block, 'shard', axis=0, tiled=True)]
  transfers between devices with their start and end apart: 14 -> 18, of which waited for: 14 -> 17; matrix products, arithmetic and copies ran while one was open for 11% -> 18% of each run, Pallas kernels for 0% -> 0%
where the time goes in v2:
time: 1450 us; the launch traced here: 1440 us
  waiting for transfers between devices  917 us (63%)
  matrix products  366 us (25%)
  other arithmetic  69.4 us (5%)
  local copies, waits for them, and re-layouts  61 us (4%)
  between operations  17.7 us (1%)
    all_gather x4, waiting for transfers between devices, renew(): return lax.all_gather(fresh, ('shard', 'rep'), axis=0, tiled=True)  292 us
    reduce_scatter x3, waiting for transfers between devices, total(): lax.psum_scatter(lengthened(part, rows), 'rep', scatter_dimension=0, tile...  200 us
    reduce_scatter x4, waiting for transfers between devices, group_total(): lax.psum_scatter(grad.astype(jnp.bfloat16), 'shard', scatter_dimension=0,...  173 us
    all_gather x4, waiting for transfers between devices, fetch(): return lax.all_gather(block, 'shard', axis=0, tiled=True)  151 us
    dot_general x53, matrix products, near(): return jnp.dot(left, right, precision=lax.Precision.HIGH)  115 us
    unnamed x18, waiting for transfers between devices  77.1 us
    dot_general x10, matrix products, product(): return jnp.dot(left, right, preferred_element_type=jnp.float32)  70.3 us
    dot_general x5, matrix products, right_product(): lax.dot_general(left, right, (((1,), (1,)), ((), ())), preferred_element_...  63.5 us
  transfers between devices with their start and end apart: 18, of which 17 were waited for; matrix products, arithmetic and copies ran while one was open for 18% of the time, Pallas kernels for 0%

profile of v2, /device:TPU:0, one launch (start us, length us, event | category | flops | bytes accessed | tf_op | source)
XLA Modules:
  0.0 1441.9 jit_solution(11020867110310692836)
XLA Ops:
  28.6 22.8 %all-gather.11.cloned.1.call-done = bf16[1024,2048]{1,0:T(8,128)(2,1)} async-done(((bf16[256,2048]{1,0:T(8,128)(2,1)}), bf16[1024,2048]{1,0:T(8,128)(2,1)}) %all-gather.11.cloned.1.call-update) | async-done | bytes 4194320 | tf_op jit(solution)/shard_map/all_gather | solution.py:143
  63.4 11.4 fusion.262
  74.8 6.7 fusion.127
  86.2 27.5 %all-gather.13.cloned.1.call-done = bf16[896,4864]{1,0:T(8,128)(2,1)} async-done(((bf16[224,4864]{1,0:T(8,128)(2,1)}), bf16[896,4864]{1,0:T(8,128)(2,1)}) %all-gather.13.cloned.1.call-update) | async-done | bytes 8716304 | tf_op jit(solution)/shard_map/all_gather | solution.py:143
  113.7 11.7 fusion.266
  125.4 50.6 %all-gather.15.cloned.1.call-done = bf16[896,4864]{1,0:T(8,128)(2,1)} async-done(((bf16[224,4864]{1,0:T(8,128)(2,1)}), bf16[896,4864]{1,0:T(8,128)(2,1)}) %all-gather.15.cloned.1.call-update) | async-done | bytes 8716304 | tf_op jit(solution)/shard_map/all_gather | solution.py:143
  176.0 11.7 fusion.267
  187.7 50.5 %all-gather.17.cloned.1.call-done = bf16[4864,896]{1,0:T(8,128)(2,1)} async-done(((bf16[1216,896]{1,0:T(8,128)(2,1)}), bf16[4864,896]{1,0:T(8,128)(2,1)}) %all-gather.17.cloned.1.call-update) | async-done | bytes 8716304 | tf_op jit(solution)/shard_map/all_gather | solution.py:143
  238.2 19.0 %multiply_convert_fusion = (bf16[512,4864]{1,0:T(8,128)(2,1)}, bf16[512,4864]{1,0:T(8,128)(2,1)}, bf16[512,4864]{1,0:T(8,128)(2,1)}) fusion(f32[512,4864]{1,0:T(8,128)} %fusion.266, f32[512,4864]{1,0:T(8,128)} %fusion.267, bf16[512,896]{1,0:T(8,128)(2,1)S(1)} %copy-done.16, bf16[4864,896]{1,0:T(8,128)(2,1)} %all-gather.17.cloned.1.call-done), kind=kOutput, calls=%fused_computation.15 | convolution fusion | flops 4500094976 | bytes 44498944 | tf_op jit(solution)/shard_map/dot_general | solution.py:46
  257.2 10.4 convolution_convert_fusion.2
  267.6 10.8 convolution_convert_fusion.1
  278.4 10.8 convolution_convert_fusion
  289.1 12.0 fusion.268
  301.2 10.8 convolution_add_fusion.1
  324.7 8.7 fusion.269
  333.4 21.7 %fusion.19 = f32[2,64,7,512]{3,1,2,0:T(8,128)} fusion(bf16[512,2,64,1]{0,2,3,1:T(8,128)(2,1)S(1)} %copy-done.23, f32[2,512,512,7]{2,1,3,0:T(8,128)} %fusion.269, f32[2,7,512,512]{2,3,1,0:T(8,128)} %get-tuple-element.78, f32[2,7,512]{2,1,0:T(8,128)S(1)} %copy-done.37), kind=kOutput, calls=%fused_computation.34 | convolution fusion | flops 495459840 | bytes 31354880 | tf_op jit(solution)/shard_map/hgqk,khd->qhgd/dot_general | solution.py:290
  358.9 21.4 %broadcast_multiply_fusion = (f32[512,2,64]{0,2,1:T(8,128)}, f32[512,2,64]{0,2,1:T(8,128)}) fusion(f32[512,64]{0,1:T(8,128)S(1)} %get-tuple-element.72, bf16[512,2,7,64]{0,3,2,1:T(8,128)(2,1)} %fusion.73, f32[2,512,512,7]{2,1,3,0:T(8,128)} %fusion.269, f32[2,7,512,512]{2,3,1,0:T(8,128)} %get-tuple-element.78, f32[2,7,512]{2,1,0:T(8,128)S(1)} %copy-done.37), kind=kOutput, calls=%fused_computation.286 | convolution fusion | flops 495525376 | bytes 30961664 | tf_op jit(solution)/shard_map/hgqk,qhgd->khd/dot_general | solution.py:293
  382.3 8.0 fusion.140
  413.2 48.9 %reduce-scatter.13.cloned.1.call-done = bf16[224,4864]{1,0:T(8,128)(2,1)} async-done(((bf16[896,4864]{1,0:T(8,128)(2,1)}), bf16[224,4864]{1,0:T(8,128)(2,1)}) %reduce-scatter.13.cloned.1.call-update) | async-done | bytes 2179088 | tf_op jit(solution)/shard_map/reduce_scatter | solution.py:147
  462.2 76.4 %reduce-scatter.15.cloned.1.call-done = bf16[224,4864]{1,0:T(8,128)(2,1)} async-done(((bf16[896,4864]{1,0:T(8,128)(2,1)}), bf16[224,4864]{1,0:T(8,128)(2,1)}) %reduce-scatter.15.cloned.1.call-update) | async-done | bytes 2179088 | tf_op jit(solution)/shard_map/reduce_scatter | solution.py:147
  538.7 47.6 %reduce-scatter.17.cloned.1.call-done = bf16[256,2048]{1,0:T(8,128)(2,1)} async-done(((bf16[1024,2048]{1,0:T(8,128)(2,1)}), bf16[256,2048]{1,0:T(8,128)(2,1)}) %reduce-scatter.17.cloned.1.call-update) | async-done | bytes 1048592 | tf_op jit(solution)/shard_map/reduce_scatter | solution.py:147
  595.7 57.7 %reduce-scatter.19.cloned.1.call-done = bf16[32,2048]{1,0:T(8,128)(2,1)} async-done(((bf16[256,2048]{1,0:T(8,128)(2,1)}), bf16[32,2048]{1,0:T(8,128)(2,1)}) %reduce-scatter.19.cloned.1.call-update) | async-done | bytes 131088 | tf_op jit(solution)/shard_map/reduce_scatter | solution.py:153
  655.3 75.1 %reduce-scatter.25.cloned.1.call-done = bf16[152,896]{1,0:T(8,128)(2,1)} async-done(((bf16[1216,896]{1,0:T(8,128)(2,1)}), bf16[152,896]{1,0:T(8,128)(2,1)}) %reduce-scatter.25.cloned.1.call-update) | async-done | bytes 272400
  732.4 71.9 %reduce-scatter.21.cloned.1.call-done = bf16[32,4864]{1,0:T(8,128)(2,1)} async-done(((bf16[256,4864]{1,0:T(8,128)(2,1)}), bf16[32,4864]{1,0:T(8,128)(2,1)}) %reduce-scatter.21.cloned.1.call-update) | async-done | bytes 311312 | tf_op jit(solution)/shard_map/reduce_scatter | solution.py:153
  806.4 70.5 %reduce-scatter.23.cloned.1.call-done = bf16[32,4864]{1,0:T(8,128)(2,1)} async-done(((bf16[256,4864]{1,0:T(8,128)(2,1)}), bf16[32,4864]{1,0:T(8,128)(2,1)}) %reduce-scatter.23.cloned.1.call-update) | async-done | bytes 311312 | tf_op jit(solution)/shard_map/reduce_scatter | solution.py:153
  882.6 10.5 add_convert_fusion
  893.2 48.7 %all-gather.19.cloned.1.call-done = bf16[1024,2048]{1,0:T(8,128)(2,1)} async-done(((bf16[32,2048]{1,0:T(8,128)(2,1)}), bf16[1024,2048]{1,0:T(8,128)(2,1)}) %all-gather.19.cloned.1.call-update) | async-done | bytes 4194320 | tf_op jit(solution)/shard_map/all_gather | solution.py:161
  953.1 69.7 %all-gather.25.cloned.1.call-done = bf16[4864,896]{1,0:T(8,128)(2,1)} async-done(((bf16[152,896]{1,0:T(8,128)(2,1)}), bf16[4864,896]{1,0:T(8,128)(2,1)}) %all-gather.25.cloned.1.call-update) | async-done | bytes 8716304 | tf_op jit(solution)/shard_map/all_gather | solution.py:161
  1022.8 86.6 %all-gather.21.cloned.1.call-done = bf16[1024,4864]{1,0:T(8,128)(2,1)} async-done(((bf16[32,4864]{1,0:T(8,128)(2,1)}), bf16[1024,4864]{1,0:T(8,128)(2,1)}) %all-gather.21.cloned.1.call-update) | async-done | bytes 9961488 | tf_op jit(solution)/shard_map/all_gather | solution.py:161
  1109.4 86.6 %all-gather.23.cloned.1.call-done = bf16[1024,4864]{1,0:T(8,128)(2,1)} async-done(((bf16[32,4864]{1,0:T(8,128)(2,1)}), bf16[1024,4864]{1,0:T(8,128)(2,1)}) %all-gather.23.cloned.1.call-update) | async-done | bytes 9961488 | tf_op jit(solution)/shard_map/all_gather | solution.py:161
  1196.0 40.9 %conditional.1 = (f32[896,896]{1,0:T(8,128)S(1)}) conditional(s32[]{:T(128)} %clamp.3, bf16[1024,4864]{1,0:T(8,128)(2,1)} %all-gather.21.cloned.1.call-done, bf16[1024,4864]{1,0:T(8,128)(2,1)} %all-gather.23.cloned.1.call-done, bf16[4864,896]{1,0:T(8,128)(2,1)} %all-gather.25.cloned.1.call-done, (pred[]{:T(512)}, ...), branch_computations={%region_20.21_spmd, %region_21.22_spmd, %region_22.23_spmd, %regio... | conditional | flops 10200547328 | bytes 35389448 | solution.py:360
  1196.0 17.8 %fusion.263 = f32[1024,1024]{1,0:T(8,128)} fusion(bf16[1024,4864]{1,0:T(8,128)(2,1)} %param), kind=kOutput, calls=%fused_computation.392 | convolution fusion | flops 10200547328 | bytes 14155776 | tf_op jit(solution)/shard_map/cond/branch_0_fun/dot_general | solution.py:46
  1244.2 6.1 multiply_add_fusion.21
  1250.3 6.4 multiply_add_fusion.20
  1262.6 6.7 multiply_add_fusion.22
  1269.4 6.0 multiply_add_fusion.14
  1275.4 6.3 multiply_add_fusion.13
  1287.6 6.4 multiply_add_fusion.7
  1294.1 6.0 multiply_add_fusion.15
  1300.1 6.2 multiply_add_fusion.6
  1312.2 6.4 multiply_add_fusion.1
  1318.7 6.0 multiply_add_fusion.8
  1324.7 6.2 multiply_add_fusion
  1336.8 7.6 multiply_convert_fusion.3
  1368.4 21.9 %all-gather.27.cloned.1.call-done = bf16[3584,896]{1,0:T(8,128)(2,1)} async-done(((bf16[896,896]{1,0:T(8,128)(2,1)}), bf16[3584,896]{1,0:T(8,128)(2,1)}) %all-gather.27.cloned.1.call-update) | async-done | bytes 6422544 | tf_op jit(solution)/shard_map/all_gather | solution.py:370
  1400.1 9.6 fusion.16
  1413.3 8.3 convolution_subtract_fusion
  1421.5 8.4 fusion.17
  (282 shorter events, 196.3 us)
Async XLA Ops:
  7.2 44.2 %all-gather.11.cloned.1.call-start = ((), (), s32[]{:S(2)}) async-start(), calls=%async_computation.8 | async-start | bytes 5242880 | tf_op jit(solution)/shard_map/all_gather | solution.py:143
  14.0 99.7 %all-gather.13.cloned.1.call-start = ((), (), s32[]{:S(2)}) async-start(), calls=%async_computation.9 | async-start | bytes 10895360 | tf_op jit(solution)/shard_map/all_gather | solution.py:143
  17.9 158.1 %all-gather.15.cloned.1.call-start = ((), (), s32[]{:S(2)}) async-start(), calls=%async_computation.10 | async-start | bytes 10895360 | tf_op jit(solution)/shard_map/all_gather | solution.py:143
  21.8 4.4 copy-start.27
  21.8 5.6 copy-start
  21.8 216.4 %all-gather.17.cloned.1.call-start = ((), (), s32[]{:S(2)}) async-start(), calls=%async_computation.11 | async-start | bytes 10895360 | tf_op jit(solution)/shard_map/all_gather | solution.py:143
  26.2 387.0 %reduce-scatter.11.cloned.1.call-start = ((), (), s32[]{:S(2)}) async-start(), calls=%async_computation.12 | async-start | bytes 10895360 | tf_op jit(solution)/shard_map/reduce_scatter | solution.py:147
  27.6 25.9 %copy-start.28 = (f32[512]{0:T(512)}, f32[512]{0:T(512)S(1)}, u32[]{:S(2)}) copy-start(f32[512]{0:T(512)S(1)} %add_rsqrt_fusion.1) | copy-start | bytes 6148
  74.8 6.7 copy-start.36
  86.1 27.5 %copy-start.17 = (bf16[512,896]{1,0:T(8,128)(2,1)}, bf16[512,896]{1,0:T(8,128)(2,1)S(1)}, u32[]{:S(2)}) copy-start(bf16[512,896]{1,0:T(8,128)(2,1)S(1)} %multiply_convert_fusion.4) | copy-start | bytes 2752516
  125.4 112.8 %copy-start.16 = (bf16[512,896]{1,0:T(8,128)(2,1)S(1)}, bf16[512,896]{1,0:T(8,128)(2,1)}, u32[]{:S(2)}) copy-start(bf16[512,896]{1,0:T(8,128)(2,1)} %param.26) | copy-start | bytes 2752516
  312.0 150.2 %reduce-scatter.13.cloned.1.call-start = ((), (), s32[]{:S(2)}) async-start(), calls=%async_computation.13 | async-start | bytes 10895360 | tf_op jit(solution)/shard_map/reduce_scatter | solution.py:147
  312.6 226.0 %reduce-scatter.15.cloned.1.call-start = ((), (), s32[]{:S(2)}) async-start(), calls=%async_computation.14 | async-start | bytes 10895360 | tf_op jit(solution)/shard_map/reduce_scatter | solution.py:147
  313.3 272.9 %reduce-scatter.17.cloned.1.call-start = ((), (), s32[]{:S(2)}) async-start(), calls=%async_computation.15 | async-start | bytes 5242880 | tf_op jit(solution)/shard_map/reduce_scatter | solution.py:147
  324.7 8.7 copy-start.23
  324.7 8.7 copy-start.37
  358.9 37.8 %copy-start.9 = (bf16[512,896]{0,1:T(8,128)(2,1)}, bf16[512,896]{0,1:T(8,128)(2,1)S(1)}, u32[]{:S(2)}) copy-start(bf16[512,896]{0,1:T(8,128)(2,1)S(1)} %fusion.75) | copy-start | bytes 2752516
  382.3 8.0 copy-start.7
  401.0 5.2 copy-start.1
  401.0 5.2 copy-start.25
  401.0 5.2 copy-start.29
  538.6 114.8 %reduce-scatter.19.cloned.1.call-start = ((), (), s32[]{:S(2)}) async-start(), calls=%async_computation.16 | async-start | bytes 1179648 | tf_op jit(solution)/shard_map/reduce_scatter | solution.py:153
  586.3 144.1 %reduce-scatter.25.cloned.1.call-start = ((), (), s32[]{:S(2)}) async-start(), calls=%async_computation.24 | async-start | bytes 2451456
  586.9 217.5 %reduce-scatter.21.cloned.1.call-start = ((), (), s32[]{:S(2)}) async-start(), calls=%async_computation.18 | async-start | bytes 2801664 | tf_op jit(solution)/shard_map/reduce_scatter | solution.py:153
  590.2 63.2 %copy-start.18 = (f32[224,896]{1,0:T(8,128)S(1)}, f32[224,896]{1,0:T(8,128)}, u32[]{:S(2)}) copy-start(f32[224,896]{1,0:T(8,128)} %param.40) | copy-start | bytes 2408452
  590.2 286.6 %reduce-scatter.23.cloned.1.call-start = ((), (), s32[]{:S(2)}) async-start(), calls=%async_computation.20 | async-start | bytes 2801664 | tf_op jit(solution)/shard_map/reduce_scatter | solution.py:153
  593.5 348.3 %all-gather.19.cloned.1.call-start = ((), (), s32[]{:S(2)}) async-start(), calls=%async_computation.17 | async-start | bytes 4325376 | tf_op jit(solution)/shard_map/all_gather | solution.py:161
  655.3 367.5 %all-gather.25.cloned.1.call-start = ((), (), s32[]{:S(2)}) async-start(), calls=%async_computation.22 | async-start | bytes 8988672 | tf_op jit(solution)/shard_map/all_gather | solution.py:161
  732.3 377.1 %all-gather.21.cloned.1.call-start = ((), (), s32[]{:S(2)}) async-start(), calls=%async_computation.19 | async-start | bytes 10272768 | tf_op jit(solution)/shard_map/all_gather | solution.py:161
  806.3 72.6 %copy-start.31 = (f32[512]{0:T(512)S(1)}, f32[512]{0:T(512)}, u32[]{:S(2)}) copy-start(f32[512]{0:T(512)} %get-tuple-element.50) | copy-start | bytes 6148
  806.3 72.6 %copy-start.26 = (f32[896]{0:T(1024)S(1)}, f32[896]{0:T(1024)}, u32[]{:S(2)}) copy-start(f32[896]{0:T(1024)} %copy-done.24) | copy-start | bytes 10756
  806.3 72.6 %copy-start.30 = (f32[512]{0:T(512)S(1)}, f32[512]{0:T(512)}, u32[]{:S(2)}) copy-start(f32[512]{0:T(512)} %copy-done.28) | copy-start | bytes 6148
  806.3 389.7 %all-gather.23.cloned.1.call-start = ((), (), s32[]{:S(2)}) async-start(), calls=%async_computation.21 | async-start | bytes 10272768 | tf_op jit(solution)/shard_map/all_gather | solution.py:161
  878.8 511.5 %all-gather.27.cloned.1.call-start = ((), (), s32[]{:S(2)}) async-start(), calls=%async_computation.23 | async-start | bytes 8028160 | tf_op jit(solution)/shard_map/all_gather | solution.py:370
  941.8 9.6 copy-start.33
  951.3 244.7 %copy-start.35 = (f32[2,224]{1,0:T(2,128)}, f32[2,224]{1,0:T(2,128)S(1)}, u32[]{:S(2)}) copy-start(f32[2,224]{1,0:T(2,128)S(1)} %reshape.319) | copy-start | bytes 5380
  951.4 393.1 %copy-start.32 = (f32[288]{0:T(512)}, f32[288]{0:T(512)S(1)}, u32[]{:S(2)}) copy-start(f32[288]{0:T(512)S(1)} %slice_reduce_fusion.2) | copy-start | bytes 3460
  1336.8 7.6 copy-start.34
  1344.4 5.8 copy-start.19
  1344.5 7.4 copy-start.20
  1355.9 75.8 %copy-start.13 = (f32[224,896]{1,0:T(8,128)}, f32[224,896]{1,0:T(8,128)S(1)}, u32[]{:S(2)}) copy-start(f32[224,896]{1,0:T(8,128)S(1)} %get-tuple-element.60) | copy-start | bytes 2408452
  1355.9 77.5 %copy-start.12 = (f32[224,896]{1,0:T(8,128)}, f32[224,896]{1,0:T(8,128)S(1)}, u32[]{:S(2)}) copy-start(f32[224,896]{1,0:T(8,128)S(1)} %get-tuple-element.59) | copy-start | bytes 2408452
  1394.2 37.5 %collective-permute-start = (bf16[896,896]{1,0:T(8,128)(2,1)}, bf16[896,896]{1,0:T(8,128)(2,1)S(1)}, u32[]{:S(2)}, u32[]{:S(2)}) collective-permute-start(bf16[896,896]{1,0:T(8,128)(2,1)} %get-tuple-element.58), channel_id=1, source_target_pairs={{0,1},{1,0},{2,3},{3,2},{4,5},{5,4},{6,7},{7,6},{8,9},{9,8},{10,11... | collective-permute-start | bytes 4816904 | tf_op jit(solution)/shard_map/ppermute | solution.py:372
  1400.1 21.4 %slice-start = ((s8[4358144]{0:T(1024)(128)(4,1)}), s8[163840]{0:T(1024)(128)(4,1)S(1)}, s32[]{:S(2)}) async-start(s8[4358144]{0:T(1024)(128)(4,1)} %bitcast.243), calls=%async_computation.25 | async-start | bytes 327680
  1413.1 18.6 %slice-start.2 = ((s8[6422528]{0:T(1024)(128)(4,1)}), s8[4194304]{0:T(1024)(128)(4,1)S(1)}, s32[]{:S(2)}) async-start(s8[6422528]{0:T(1024)(128)(4,1)} %bitcast.250), calls=%async_computation.27 | async-start | bytes 8388608
  1413.2 8.3 slice-start.1
  1413.2 18.5 %slice-start.3 = ((s8[6422528]{0:T(1024)(128)(4,1)}), s8[2228224]{0:T(1024)(128)(4,1)S(1)}, s32[]{:S(2)}) async-start(s8[6422528]{0:T(1024)(128)(4,1)} %bitcast.250), calls=%async_computation.28 | async-start | bytes 4456448
  1421.5 10.2 copy-start.10
  (12 other events, 25.1 us)
Sparse Core Ops, SparseCore 0:
  14.2 37.1 all-gather.10
  53.5 60.1 all-gather.12
  115.8 60.1 all-gather.14
  178.0 60.1 all-gather.16
  312.1 73.7 reduce-scatter.10
  388.4 73.7 reduce-scatter.12
  464.8 73.7 reduce-scatter.14
  541.7 44.5 reduce-scatter.16
  590.0 63.3 reduce-scatter.18
  656.7 73.6 reduce-scatter.24
  734.9 69.3 reduce-scatter.20
  808.3 68.5 reduce-scatter.22
  880.8 60.9 all-gather.18
  945.5 77.2 all-gather.24
  1026.4 82.9 all-gather.20
  1113.1 82.8 all-gather.22
  1344.6 45.6 all-gather.26
